TPU v7x, 512 devices: a whole 4x8x8 slice. The times are simulated.
512 devices in a mesh: dp: 4 (over x), row: 8 (over y_lo, core), col: 16 (over z, y_hi).
Axes of the slice: x: 4, y: 8 (y_hi: 2, y_lo: 4; y = y_hi * 4 + y_lo), z: 8, core: 2. Of those that a mesh axis runs over, the one named last changes fastest.
Arguments:
- tokens_window: bfloat16 [16384, 2048], P(('dp', 'row'), 'col'), parts along dimension 0, may hold values from -6 to 6
- weight_window: bfloat16 [2048, 24576], P('row', 'col'), may hold values from -0.125 to 0.125
- accumulated: float32 [16384, 24576], P(('dp', 'row'), 'col'), parts along dimension 0, may hold values from -6 to 6
Outputs:
- activated: bfloat16 [16384, 24576], P(('dp', 'row'), 'col'), parts along dimension 0
There are 4 independent parts, one for each index of `dp`. A program takes and returns all parts, laid end to end along the dimension named above; an argument that names none is the same for every part. Nothing has to cross between parts.
All inputs are finite; a program needn't handle non-finite values.
Results may differ from a plain program's by a relative error of at most 0.001.
Values may be sent and summed in bfloat16 or wider, within the bound.
No kernel may reach another device: no remote copies, remote signals or barrier semaphores. Data moves between devices by JAX's collectives and lax.ppermute only.
A program may use at most 64 MiB of HBM per device.

v0:
```python
import jax
import jax.numpy as jnp
from jax import lax
from jax.sharding import PartitionSpec as P


def shards(tokens_window, weight_window, accumulated):
    weight_rows = lax.all_gather(weight_window, "row", axis=0, tiled=True)
    total = accumulated + jnp.dot(
        lax.all_gather(tokens_window, "col", axis=1, tiled=True),
        weight_rows,
        preferred_element_type=jnp.float32,
    )
    return jax.nn.gelu(total, approximate=True).astype(jnp.bfloat16)


def solution(mesh):
    return jax.shard_map(
        shards,
        mesh=mesh,
        in_specs=(P(("dp", "row"), "col"), P("row", "col"), P(("dp", "row"), "col")),
        out_specs=P(("dp", "row"), "col"),
        check_vma=False,
    )
```

profile of v0, /device:TPU:1, one launch (start us, length us, event | category | flops | bytes accessed | tf_op | source)
XLA Modules:
  0.0 208.5 jit_solution(17915001794838020742)
XLA Ops:
  6.5 0.0 all-gather.3.cloned.1.call-start
  6.5 0.7 all-gather.3.cloned.1.call-update
  7.3 0.0 all-gather.5.cloned.1.call-start
  7.3 0.7 all-gather.5.cloned.1.call-update
  8.0 105.7 %all-gather.3.cloned.1.call-done = bf16[512,2048]{1,0:T(8,128)(2,1)} async-done(((bf16[512,128]{1,0:T(8,128)(2,1)}), bf16[512,2048]{1,0:T(8,128)(2,1)}) %all-gather.3.cloned.1.call-update) | async-done | bytes 2097168 | tf_op jit(solution)/shard_map/all_gather | solution.py:10
  113.7 78.6 %all-gather.5.cloned.1.call-done = bf16[2048,1536]{1,0:T(8,128)(2,1)} async-done(((bf16[256,1536]{1,0:T(8,128)(2,1)}), bf16[2048,1536]{1,0:T(8,128)(2,1)}) %all-gather.5.cloned.1.call-update) | async-done | bytes 6291472 | tf_op jit(solution)/shard_map/all_gather | solution.py:8
  192.3 9.4 %fusion.7 = bf16[512,1536]{1,0:T(8,128)(2,1)} fusion(f32[512,1536]{1,0:T(8,128)} %param.5, bf16[512,2048]{1,0:T(8,128)(2,1)} %all-gather.3.cloned.1.call-done, bf16[2048,1536]{1,0:T(8,128)(2,1)} %all-gather.5.cloned.1.call-done), kind=kOutput, calls=%fused_computation.9 | convolution fusion | flops 3229089792 | bytes 13107200 | tf_op jit(solution)/shard_map/dot_general | solution.py:9
Async XLA Ops:
  6.5 107.1 %all-gather.3.cloned.1.call-start = ((), (), s32[]{:S(2)}) async-start(), calls=%async_computation | async-start | bytes 2228224 | tf_op jit(solution)/shard_map/all_gather | solution.py:10
  7.3 185.0 %all-gather.5.cloned.1.call-start = ((), (), s32[]{:S(2)}) async-start(), calls=%async_computation.1 | async-start | bytes 7077888 | tf_op jit(solution)/shard_map/all_gather | solution.py:8
Sparse Core Ops, SparseCore 0:
  10.4 103.2 all-gather.2
  115.7 76.4 all-gather.4
where the time goes:
time: 210 us; the launch traced here: 209 us
  waiting for transfers between devices  186 us (89%)
  between operations  13.4 us (6%)
  matrix products  9.43 us (4%)
    all_gather x1, waiting for transfers between devices, shards(): lax.all_gather(tokens_window, 'col', axis=1, tiled=True)  106 us
    all_gather x1, waiting for transfers between devices, shards(): weight_rows = lax.all_gather(weight_window, 'row', axis=0, tiled=True)  78.6 us
    dot_general x1, matrix products, shards(): jnp.dot(lax.all_gather(tokens_window, 'col', axis=1, tiled=True), weight_...  9.43 us
  transfers between devices with their start and end apart: 2, of which 2 were waited for; matrix products, arithmetic and copies ran while one was open for 0% of the time, Pallas kernels for 0%

commit v1 on v0

v1 whole, which is shorter than its diff:
```python
import functools

import jax
import jax.numpy as jnp
from jax import lax
from jax.experimental import pallas as pl
from jax.experimental.pallas import tpu as pltpu
from jax.sharding import PartitionSpec as P

AXES = ("dp", "row", "col")
X, YL, CORES, Z, YH = 4, 4, 2, 8, 2
TOK, KB, FF = 512, 256, 1536
Q = FF // X
HALF = KB // YH


def send(array, to):
    pairs = []
    for x in range(X):
        for yl in range(YL):
            for c in range(CORES):
                for z in range(Z):
                    for yh in range(YH):
                        x2, yl2, c2, z2, yh2 = to(x, yl, c, z, yh)
                        source = (x * YL * CORES + yl * CORES + c) * Z * YH + z * YH + yh
                        target = ((x2 % X) * YL * CORES + yl2 * CORES + c2) * Z * YH + (z2 % Z) * YH + yh2
                        pairs.append((source, target))
    return lax.ppermute(array, AXES, pairs)


def swap(array):
    return send(array, lambda x, yl, c, z, yh: (x, yl, 1 - c, z, yh))


def gelu(v):
    return 0.5 * v * (1.0 + jnp.tanh(0.7978845608028654 * (v + 0.044715 * (v * v * v))))


def kernel(place, *refs):
    (t, t1, t2, t3, vp, vm, p2, m2, w, sw, g, sg, x1, x2, x3, s1, s2, s3, acc, out,
     tokens, weights, sums, result, t_sem, w_sem, a_sem, o_sem) = refs
    d, yl, c, z, yh = (place[i] for i in range(5))

    def start(source, target, sem):
        copy = pltpu.make_async_copy(source, target, sem)
        copy.start()
        return copy

    t_copies = []
    parts = [(t, 0, 0, 0), (t1, 0, 0, 1), (t2, 0, 4, 0), (t3, 0, 4, 1)]
    for v, dz in ((vp, 1), (vm, 7)):
        parts += [(v, 0, dz, 0), (v, 1, dz, 1), (v, 2, dz + 4, 0), (v, 3, dz + 4, 1)]
    for v, dz in ((p2, 2), (m2, 6)):
        parts += [(v, 0, dz, 0), (v, 1, dz, 1)]
    for i, (ref, column, dz, dyh) in enumerate(parts):
        at = pl.multiple_of((lax.rem(z + dz, Z) * YH + (yh + dyh - 2 * yh * dyh)) * HALF, HALF)
        t_copies.append(start(ref.at[:, pl.ds(column * HALF, HALF)], tokens.at[:, pl.ds(at, HALF)], t_sem.at[i]))

    w_copies, a_copies = [], []
    for j, (mine, other) in enumerate(((g, sg), (x1, s1), (x2, s2), (x3, s3))):
        column = pl.multiple_of(lax.bitwise_xor(d, j) * Q, 128)
        a_copies.append(start(acc.at[:, pl.ds(column, Q)], sums.at[j], a_sem.at[j]))
        copies = []
        for side, (own, rest) in enumerate(((w, mine), (sw, other))):
            core = c if side == 0 else 1 - c
            for k in range(YL):
                row = pl.multiple_of((lax.bitwise_xor(yl, k) * CORES + core) * KB, KB)
                source = own.at[:, pl.ds(column, Q)] if k == 0 else rest.at[pl.ds((k - 1) * KB, KB), :]
                copies.append(start(source, weights.at[j, pl.ds(row, KB), :], w_sem.at[j * 8 + side * 4 + k]))
        w_copies.append(copies)

    for copy in t_copies:
        copy.wait()
    o_copies = []
    for j in range(X):
        for copy in w_copies[j]:
            copy.wait()
        a_copies[j].wait()
        total = sums[j] + jnp.dot(tokens[...], weights[j], preferred_element_type=jnp.float32)
        result[j] = gelu(total).astype(jnp.bfloat16)
        column = pl.multiple_of(lax.bitwise_xor(d, j) * Q, 128)
        o_copies.append(start(result.at[j], out.at[:, pl.ds(column, Q)], o_sem.at[j]))
    for copy in o_copies:
        copy.wait()


def shards(t, w, acc):
    d, r, col = lax.axis_index("dp"), lax.axis_index("row"), lax.axis_index("col")
    place = jnp.stack([d, r // CORES, r % CORES, col // YH, col % YH]).astype(jnp.int32)

    mine = lax.dynamic_slice(w, (0, d * Q), (KB, Q))
    ys = [send(mine, lambda x, yl, c, z, yh, k=k: (x, yl ^ k, c, z, yh)) for k in (1, 2, 3)]
    t1 = send(t, lambda x, yl, c, z, yh: (x, yl, c, z, 1 - yh))
    t2 = send(t, lambda x, yl, c, z, yh: (x, yl, c, z + 4, yh))
    t3 = send(t, lambda x, yl, c, z, yh: (x, yl, c, z + 4, 1 - yh))
    sw = swap(w)

    g = jnp.concatenate(ys, axis=0)
    xs = [send(g, lambda x, yl, c, z, yh, j=j: (x ^ j, yl, c, z, yh)) for j in (2, 1, 3)]
    xs = [xs[1], xs[0], xs[2]]
    pair = jnp.concatenate([t, t1], axis=1)
    p2 = send(pair, lambda x, yl, c, z, yh: (x, yl, c, z - 2, yh))
    m2 = send(pair, lambda x, yl, c, z, yh: (x, yl, c, z + 2, yh))
    four = jnp.concatenate([t, t1, t2, t3], axis=1)
    vp = send(four, lambda x, yl, c, z, yh: (x, yl, c, z - 1, yh))
    vm = send(four, lambda x, yl, c, z, yh: (x, yl, c, z + 1, yh))
    sg = swap(g)
    ss = [swap(a) for a in xs]

    return pl.pallas_call(
        kernel,
        out_shape=jax.ShapeDtypeStruct((TOK, FF), jnp.bfloat16),
        in_specs=[pl.BlockSpec(memory_space=pltpu.SMEM)] + [pl.BlockSpec(memory_space=pl.ANY)] * 19,
        out_specs=pl.BlockSpec(memory_space=pl.ANY),
        scratch_shapes=[
            pltpu.VMEM((TOK, Z * KB), jnp.bfloat16),
            pltpu.VMEM((X, Z * KB, Q), jnp.bfloat16),
            pltpu.VMEM((X, TOK, Q), jnp.float32),
            pltpu.VMEM((X, TOK, Q), jnp.bfloat16),
            pltpu.SemaphoreType.DMA((16,)),
            pltpu.SemaphoreType.DMA((32,)),
            pltpu.SemaphoreType.DMA((X,)),
            pltpu.SemaphoreType.DMA((X,)),
        ],
        compiler_params=pltpu.CompilerParams(vmem_limit_bytes=32 * 1024 * 1024),
        cost_estimate=pl.CostEstimate(
            flops=2 * TOK * FF * Z * KB, bytes_accessed=13 * 1024 * 1024, transcendentals=TOK * FF
        ),
    )(place, t, t1, t2, t3, vp, vm, p2, m2, w, sw, g, sg, *xs, *ss, acc)


def solution(mesh):
    return jax.shard_map(
        shards,
        mesh=mesh,
        in_specs=(P(("dp", "row"), "col"), P("row", "col"), P(("dp", "row"), "col")),
        out_specs=P(("dp", "row"), "col"),
        check_vma=False,
    )
```

time: 210 us -> 110 us (0.52)
  waiting for transfers between devices: 186 us -> 13.4 us
  starting transfers between devices: 0.04 us -> 70.3 us
  local copies, waits for them, and re-layouts: 0 us -> 13.7 us
  between operations: 13.4 us -> 0.4 us
  Pallas kernels: 0 us -> 11.4 us
  matrix products: 9.43 us -> 0 us
    all_gather x2 -> x0, waiting for transfers between devices: 184 us -> none  [the longest x1 106 us: shards(): lax.all_gather(tokens_window, 'col', axis=1, tiled=True)]
    ppermute x0 -> x18, starting transfers between devices: none -> 70.3 us  [send(): return lax.ppermute(array, AXES, pairs)]
    ppermute x0 -> x18, waiting for transfers between devices: none -> 13.4 us  [send(): return lax.ppermute(array, AXES, pairs)]
    unnamed x0 -> x34, local copies, waits for them, and re-layouts: none -> 12.6 us
    pallas_call x0 -> x1, Pallas kernels: none -> 11.4 us  [shards(): pl.pallas_call(kernel, out_shape=jax.ShapeDtypeStruct((TOK, FF), jnp.bflo...]
    dot_general x1 -> x0, matrix products: 9.43 us -> none  [shards(): jnp.dot(lax.all_gather(tokens_window, 'col', axis=1, tiled=True), weight_...]
  transfers between devices with their start and end apart: 2 -> 18, of which waited for: 2 -> 4; matrix products, arithmetic and copies ran while one was open for 0% -> 2% of each run, Pallas kernels for 0% -> 0%
where the time goes in v1:
time: 110 us; the launch traced here: 109 us
  starting transfers between devices  70.3 us (64%)
  local copies, waits for them, and re-layouts  13.7 us (12%)
  waiting for transfers between devices  13.4 us (12%)
  Pallas kernels  11.4 us (10%)
    ppermute x18, starting transfers between devices, send(): return lax.ppermute(array, AXES, pairs)  70.3 us
    ppermute x18, waiting for transfers between devices, send(): return lax.ppermute(array, AXES, pairs)  13.4 us
    unnamed x34, local copies, waits for them, and re-layouts  12.6 us
    pallas_call x1, Pallas kernels, shards(): pl.pallas_call(kernel, out_shape=jax.ShapeDtypeStruct((TOK, FF), jnp.bflo...  11.4 us
  transfers between devices with their start and end apart: 18, of which 4 were waited for; matrix products, arithmetic and copies ran while one was open for 2% of the time, Pallas kernels for 0%

profile of v1, /device:TPU:1, one launch (start us, length us, event | category | flops | bytes accessed | tf_op | source)
XLA Modules:
  0.0 109.2 jit_solution(7886752256795483028)
XLA Ops:
  0.0 16.8 %collective-permute-start.2 = (bf16[512,128]{1,0:T(8,128)(2,1)}, bf16[512,128]{1,0:T(8,128)(2,1)S(1)}, u32[]{:S(2)}, u32[]{:S(2)}) collective-permute-start(bf16[512,128]{1,0:T(8,128)(2,1)} %refs_0_.1), channel_id=1, source_target_pairs={{0,9},{1,8},{2,11},{3,10},{4,13},{5,12},{6,15},{7,14},{8,1},{9,0},... | collective-permute-start | bytes 393224 | tf_op jit(solution)/shard_map/ppermute | solution.py:28
  16.9 1.9 %collective-permute-start.1 = (bf16[512,128]{1,0:T(8,128)(2,1)}, bf16[512,128]{1,0:T(8,128)(2,1)S(1)}, u32[]{:S(2)}, u32[]{:S(2)}) collective-permute-start(bf16[512,128]{1,0:T(8,128)(2,1)} %refs_0_.1), channel_id=1, source_target_pairs={{0,8},{1,9},{2,10},{3,11},{4,12},{5,13},{6,14},{7,15},{8,0},{9,1},... | collective-permute-start | bytes 393224 | tf_op jit(solution)/shard_map/ppermute | solution.py:28
  18.8 2.2 %collective-permute-start = (bf16[512,128]{1,0:T(8,128)(2,1)}, bf16[512,128]{1,0:T(8,128)(2,1)S(1)}, u32[]{:S(2)}, u32[]{:S(2)}) collective-permute-start(bf16[512,128]{1,0:T(8,128)(2,1)} %refs_0_.1), channel_id=1, source_target_pairs={{0,1},{1,0},{2,3},{3,2},{4,5},{5,4},{6,7},{7,6},{8,9},{9,8},{10,11... | collective-permute-start | bytes 393224 | tf_op jit(solution)/shard_map/ppermute | solution.py:28
  21.0 1.0 constant_dynamic-slice_fusion
  22.0 4.8 %collective-permute-start.10 = (bf16[256,384]{1,0:T(8,128)(2,1)S(1)}, bf16[256,384]{1,0:T(8,128)(2,1)S(1)}, u32[]{:S(2)}, u32[]{:S(2)}) collective-permute-start(bf16[256,384]{1,0:T(8,128)(2,1)S(1)} %constant_dynamic-slice_fusion), channel_id=1, source_target_pairs={{0,96},{1,97},{2,98},{3,99},{4,100},{5,101},{6,102},{7,103},{8,104... | collective-permute-start | bytes 589832 | tf_op jit(solution)/shard_map/ppermute | solution.py:28
  26.7 1.9 %collective-permute-start.9 = (bf16[256,384]{1,0:T(8,128)(2,1)S(1)}, bf16[256,384]{1,0:T(8,128)(2,1)S(1)}, u32[]{:S(2)}, u32[]{:S(2)}) collective-permute-start(bf16[256,384]{1,0:T(8,128)(2,1)S(1)} %constant_dynamic-slice_fusion), channel_id=1, source_target_pairs={{0,64},{1,65},{2,66},{3,67},{4,68},{5,69},{6,70},{7,71},{8,72},{9,... | collective-permute-start | bytes 589832 | tf_op jit(solution)/shard_map/ppermute | solution.py:28
  28.7 0.9 constant_dynamic-update-slice_fusion.5
  29.6 3.8 %collective-permute-done.refs_1_ = bf16[512,128]{1,0:T(8,128)(2,1)S(1)} collective-permute-done((bf16[512,128]{1,0:T(8,128)(2,1)}, bf16[512,128]{1,0:T(8,128)(2,1)S(1)}, u32[]{:S(2)}, u32[]{:S(2)}) %collective-permute-start) | collective-permute-done | bytes 131104 | tf_op jit(solution)/shard_map/ppermute | solution.py:28
  33.4 1.9 %collective-permute-start.8 = (bf16[256,384]{1,0:T(8,128)(2,1)S(1)}, bf16[256,384]{1,0:T(8,128)(2,1)S(1)}, u32[]{:S(2)}, u32[]{:S(2)}) collective-permute-start(bf16[256,384]{1,0:T(8,128)(2,1)S(1)} %constant_dynamic-slice_fusion), channel_id=1, source_target_pairs={{0,32},{1,33},{2,34},{3,35},{4,36},{5,37},{6,38},{7,39},{8,40},{9,... | collective-permute-start | bytes 589832 | tf_op jit(solution)/shard_map/ppermute | solution.py:28
  35.4 0.1 constant_dynamic-update-slice_fusion.4
  35.4 0.0 collective-permute-done.1.refs_2_
  35.4 4.1 %collective-permute-start.6 = (bf16[512,256]{1,0:T(8,128)(2,1)S(1)}, bf16[512,256]{1,0:T(8,128)(2,1)S(1)}, u32[]{:S(2)}, u32[]{:S(2)}) collective-permute-start(bf16[512,256]{1,0:T(8,128)(2,1)S(1)} %get-tuple-element.5), channel_id=1, source_target_pairs={{0,4},{1,5},{2,6},{3,7},{4,8},{5,9},{6,10},{7,11},{8,12},{9,13},{1... | collective-permute-start | bytes 786440 | tf_op jit(solution)/shard_map/ppermute | solution.py:28
  39.6 0.0 collective-permute-done.2.refs_3_
  39.6 3.3 %collective-permute-start.5 = (bf16[512,256]{1,0:T(8,128)(2,1)S(1)}, bf16[512,256]{1,0:T(8,128)(2,1)S(1)}, u32[]{:S(2)}, u32[]{:S(2)}) collective-permute-start(bf16[512,256]{1,0:T(8,128)(2,1)S(1)} %get-tuple-element.5), channel_id=1, source_target_pairs={{0,12},{1,13},{2,14},{3,15},{4,0},{5,1},{6,2},{7,3},{8,4},{9,5},{1... | collective-permute-start | bytes 786440 | tf_op jit(solution)/shard_map/ppermute | solution.py:28
  42.9 0.0 collective-permute-done.8
  43.0 2.9 %collective-permute-start.4 = (bf16[512,512]{1,0:T(8,128)(2,1)S(1)}, bf16[512,512]{1,0:T(8,128)(2,1)S(1)}, u32[]{:S(2)}, u32[]{:S(2)}) collective-permute-start(bf16[512,512]{1,0:T(8,128)(2,1)S(1)} %constant_dynamic-update-slice_fusion), channel_id=1, source_target_pairs={{0,2},{1,3},{2,4},{3,5},{4,6},{5,7},{6,8},{7,9},{8,10},{9,11},{10,... | collective-permute-start | bytes 1572872 | tf_op jit(solution)/shard_map/ppermute | solution.py:28
  45.9 1.8 %collective-permute-done.9 = bf16[256,384]{1,0:T(8,128)(2,1)S(1)} collective-permute-done((bf16[256,384]{1,0:T(8,128)(2,1)S(1)}, bf16[256,384]{1,0:T(8,128)(2,1)S(1)}, u32[]{:S(2)}, u32[]{:S(2)}) %collective-permute-start.9) | collective-permute-done | bytes 196640 | tf_op jit(solution)/shard_map/ppermute | solution.py:28
  47.7 0.0 collective-permute-done.10
  47.8 4.4 %collective-permute-start.14 = (bf16[768,384]{1,0:T(8,128)(2,1)S(1)}, bf16[768,384]{1,0:T(8,128)(2,1)S(1)}, u32[]{:S(2)}, u32[]{:S(2)}) collective-permute-start(bf16[768,384]{1,0:T(8,128)(2,1)S(1)} %constant_dynamic-update-slice_fusion.6.refs_10_), channel_id=1, source_target_pairs={{0,384},{1,385},{2,386},{3,387},{4,388},{5,389},{6,390},{7,391},{8... | collective-permute-start | bytes 1769480 | tf_op jit(solution)/shard_map/ppermute | solution.py:28
  52.2 2.4 %collective-permute-start.13 = (bf16[768,384]{1,0:T(8,128)(2,1)S(1)}, bf16[768,384]{1,0:T(8,128)(2,1)S(1)}, u32[]{:S(2)}, u32[]{:S(2)}) collective-permute-start(bf16[768,384]{1,0:T(8,128)(2,1)S(1)} %constant_dynamic-update-slice_fusion.6.refs_10_), channel_id=1, source_target_pairs={{0,256},{1,257},{2,258},{3,259},{4,260},{5,261},{6,262},{7,263},{8... | collective-permute-start | bytes 1769480 | tf_op jit(solution)/shard_map/ppermute | solution.py:28
  54.6 0.0 collective-permute-done.6.refs_7_
  54.6 0.7 copy-done.11
  55.3 2.2 %collective-permute-start.12 = (bf16[768,384]{1,0:T(8,128)(2,1)S(1)}, bf16[768,384]{1,0:T(8,128)(2,1)}, u32[]{:S(2)}, u32[]{:S(2)}) collective-permute-start(bf16[768,384]{1,0:T(8,128)(2,1)S(1)} %constant_dynamic-update-slice_fusion.6.refs_10_), channel_id=1, source_target_pairs={{0,128},{1,129},{2,130},{3,131},{4,132},{5,133},{6,134},{7,135},{8... | collective-permute-start | bytes 1769480 | tf_op jit(solution)/shard_map/ppermute | solution.py:28
  57.5 0.7 copy-done.13
  58.2 7.6 %collective-permute-start.3 = (bf16[512,512]{1,0:T(8,128)(2,1)S(1)}, bf16[512,512]{1,0:T(8,128)(2,1)S(1)}, u32[]{:S(2)}, u32[]{:S(2)}) collective-permute-start(bf16[512,512]{1,0:T(8,128)(2,1)S(1)} %constant_dynamic-update-slice_fusion), channel_id=1, source_target_pairs={{0,14},{1,15},{2,0},{3,1},{4,2},{5,3},{6,4},{7,5},{8,6},{9,7},{10,... | collective-permute-start | bytes 1572872 | tf_op jit(solution)/shard_map/ppermute | solution.py:28
  65.8 0.0 collective-permute-done.4.refs_5_
  65.8 0.8 copy-done.7
  66.6 3.5 %collective-permute-start.7 = (bf16[256,1536]{1,0:T(8,128)(2,1)}, bf16[256,1536]{1,0:T(8,128)(2,1)S(1)}, u32[]{:S(2)}, u32[]{:S(2)}) collective-permute-start(bf16[256,1536]{1,0:T(8,128)(2,1)} %refs_8_.1), channel_id=1, source_target_pairs={{0,16},{1,17},{2,18},{3,19},{4,20},{5,21},{6,22},{7,23},{8,24},{9,... | collective-permute-start | bytes 2359304 | tf_op jit(solution)/shard_map/ppermute | solution.py:28
  70.1 5.5 %collective-permute-done.3.refs_4_ = bf16[512,512]{1,0:T(8,128)(2,1)S(1)} collective-permute-done((bf16[512,512]{1,0:T(8,128)(2,1)S(1)}, bf16[512,512]{1,0:T(8,128)(2,1)S(1)}, u32[]{:S(2)}, u32[]{:S(2)}) %collective-permute-start.3) | collective-permute-done | bytes 524320 | tf_op jit(solution)/shard_map/ppermute | solution.py:28
  75.6 0.8 copy-done.9
  76.4 4.2 %collective-permute-start.11 = (bf16[768,384]{1,0:T(8,128)(2,1)S(1)}, bf16[768,384]{1,0:T(8,128)(2,1)}, u32[]{:S(2)}, u32[]{:S(2)}) collective-permute-start(bf16[768,384]{1,0:T(8,128)(2,1)S(1)} %constant_dynamic-update-slice_fusion.6.refs_10_), channel_id=1, source_target_pairs={{0,16},{1,17},{2,18},{3,19},{4,20},{5,21},{6,22},{7,23},{8,24},{9,... | collective-permute-start | bytes 1769480 | tf_op jit(solution)/shard_map/ppermute | solution.py:28
  80.6 0.0 collective-permute-done.14.refs_14_
  80.6 1.9 %collective-permute-start.17 = (bf16[768,384]{1,0:T(8,128)(2,1)S(1)}, bf16[768,384]{1,0:T(8,128)(2,1)}, u32[]{:S(2)}, u32[]{:S(2)}) collective-permute-start(bf16[768,384]{1,0:T(8,128)(2,1)S(1)} %collective-permute-done.14.refs_14_), channel_id=1, source_target_pairs={{0,16},{1,17},{2,18},{3,19},{4,20},{5,21},{6,22},{7,23},{8,24},{9,... | collective-permute-start | bytes 1769480 | tf_op jit(solution)/shard_map/ppermute | solution.py:28
  82.5 0.0 collective-permute-done.13.refs_13_
  82.5 2.4 %collective-permute-start.16 = (bf16[768,384]{1,0:T(8,128)(2,1)S(1)}, bf16[768,384]{1,0:T(8,128)(2,1)}, u32[]{:S(2)}, u32[]{:S(2)}) collective-permute-start(bf16[768,384]{1,0:T(8,128)(2,1)S(1)} %collective-permute-done.13.refs_13_), channel_id=1, source_target_pairs={{0,16},{1,17},{2,18},{3,19},{4,20},{5,21},{6,22},{7,23},{8,24},{9,... | collective-permute-start | bytes 1769480 | tf_op jit(solution)/shard_map/ppermute | solution.py:28
  84.9 0.0 collective-permute-done.12.refs_12_
  84.9 1.9 %collective-permute-start.15 = (bf16[768,384]{1,0:T(8,128)(2,1)}, bf16[768,384]{1,0:T(8,128)(2,1)}, u32[]{:S(2)}, u32[]{:S(2)}) collective-permute-start(bf16[768,384]{1,0:T(8,128)(2,1)} %collective-permute-done.12.refs_12_), channel_id=1, source_target_pairs={{0,16},{1,17},{2,18},{3,19},{4,20},{5,21},{6,22},{7,23},{8,24},{9,... | collective-permute-start | bytes 1769480 | tf_op jit(solution)/shard_map/ppermute | solution.py:28
  86.9 0.1 stack.23.place
  87.0 2.2 %collective-permute-done.15.refs_15_ = bf16[768,384]{1,0:T(8,128)(2,1)} collective-permute-done((bf16[768,384]{1,0:T(8,128)(2,1)}, bf16[768,384]{1,0:T(8,128)(2,1)}, u32[]{:S(2)}, u32[]{:S(2)}) %collective-permute-start.15) | collective-permute-done | bytes 589856 | tf_op jit(solution)/shard_map/ppermute | solution.py:28
  89.2 1.9 %copy-done = f32[512,1536]{1,0:T(8,128)S(1)} copy-done((f32[512,1536]{1,0:T(8,128)S(1)}, f32[512,1536]{1,0:T(8,128)}, u32[]{:S(2)}) %copy-start) | copy-done | bytes 3145752
  91.1 0.9 copy-done.2
  92.0 0.9 copy-done.4
  92.9 0.9 copy-done.6
  93.8 1.0 copy-done.8
  94.8 1.0 copy-done.10
  95.9 0.9 copy-done.12
  96.8 0.9 copy-done.14
  97.8 11.4 %shard_map.37 = bf16[512,1536]{1,0:T(8,128)(2,1)} custom-call(s32[5]{0:T(128)S(1)} %stack.23.place, bf16[512,128]{1,0:T(8,128)(2,1)S(1)} %copy-done.2, bf16[512,128]{1,0:T(8,128)(2,1)S(1)} %collective-permute-done.refs_1_, bf16[512,128]{1,0:T(8,128)(2,1)S(1)} %copy-done.6, bf16[512,128]{1,0:T(8,128)(2,1)S(1)} %copy-done.4, bf16[512,512]{1,0:T(8,128)(2,1)S(1)} %copy-done.10, ...), custom_call_target="tpu_custom_call" | custom-call | flops 3221225472 | bytes 13631488 | tf_op jit(solution)/shard_map/pallas_call | solution.py:110
  (28 shorter events, 0.2 us)
Async XLA Ops:
  0.0 89.2 %copy-start.1 = (bf16[256,1536]{1,0:T(8,128)(2,1)S(1)}, bf16[256,1536]{1,0:T(8,128)(2,1)}, u32[]{:S(2)}) copy-start(bf16[256,1536]{1,0:T(8,128)(2,1)} %refs_8_.1) | copy-start | bytes 2359300
  0.0 39.6 %collective-permute-start.2 = (bf16[512,128]{1,0:T(8,128)(2,1)}, bf16[512,128]{1,0:T(8,128)(2,1)S(1)}, u32[]{:S(2)}, u32[]{:S(2)}) collective-permute-start(bf16[512,128]{1,0:T(8,128)(2,1)} %refs_0_.1), channel_id=1, source_target_pairs={{0,9},{1,8},{2,11},{3,10},{4,13},{5,12},{6,15},{7,14},{8,1},{9,0},... | collective-permute-start | bytes 393224 | tf_op jit(solution)/shard_map/ppermute | solution.py:28
  16.9 18.6 %collective-permute-start.1 = (bf16[512,128]{1,0:T(8,128)(2,1)}, bf16[512,128]{1,0:T(8,128)(2,1)S(1)}, u32[]{:S(2)}, u32[]{:S(2)}) collective-permute-start(bf16[512,128]{1,0:T(8,128)(2,1)} %refs_0_.1), channel_id=1, source_target_pairs={{0,8},{1,9},{2,10},{3,11},{4,12},{5,13},{6,14},{7,15},{8,0},{9,1},... | collective-permute-start | bytes 393224 | tf_op jit(solution)/shard_map/ppermute | solution.py:28
  18.8 14.6 %collective-permute-start = (bf16[512,128]{1,0:T(8,128)(2,1)}, bf16[512,128]{1,0:T(8,128)(2,1)S(1)}, u32[]{:S(2)}, u32[]{:S(2)}) collective-permute-start(bf16[512,128]{1,0:T(8,128)(2,1)} %refs_0_.1), channel_id=1, source_target_pairs={{0,1},{1,0},{2,3},{3,2},{4,5},{5,4},{6,7},{7,6},{8,9},{9,8},{10,11... | collective-permute-start | bytes 393224 | tf_op jit(solution)/shard_map/ppermute | solution.py:28
  22.0 25.8 %collective-permute-start.10 = (bf16[256,384]{1,0:T(8,128)(2,1)S(1)}, bf16[256,384]{1,0:T(8,128)(2,1)S(1)}, u32[]{:S(2)}, u32[]{:S(2)}) collective-permute-start(bf16[256,384]{1,0:T(8,128)(2,1)S(1)} %constant_dynamic-slice_fusion), channel_id=1, source_target_pairs={{0,96},{1,97},{2,98},{3,99},{4,100},{5,101},{6,102},{7,103},{8,104... | collective-permute-start | bytes 589832 | tf_op jit(solution)/shard_map/ppermute | solution.py:28
  26.7 20.9 %collective-permute-start.9 = (bf16[256,384]{1,0:T(8,128)(2,1)S(1)}, bf16[256,384]{1,0:T(8,128)(2,1)S(1)}, u32[]{:S(2)}, u32[]{:S(2)}) collective-permute-start(bf16[256,384]{1,0:T(8,128)(2,1)S(1)} %constant_dynamic-slice_fusion), channel_id=1, source_target_pairs={{0,64},{1,65},{2,66},{3,67},{4,68},{5,69},{6,70},{7,71},{8,72},{9,... | collective-permute-start | bytes 589832 | tf_op jit(solution)/shard_map/ppermute | solution.py:28
  33.4 9.5 %collective-permute-start.8 = (bf16[256,384]{1,0:T(8,128)(2,1)S(1)}, bf16[256,384]{1,0:T(8,128)(2,1)S(1)}, u32[]{:S(2)}, u32[]{:S(2)}) collective-permute-start(bf16[256,384]{1,0:T(8,128)(2,1)S(1)} %constant_dynamic-slice_fusion), channel_id=1, source_target_pairs={{0,32},{1,33},{2,34},{3,35},{4,36},{5,37},{6,38},{7,39},{8,40},{9,... | collective-permute-start | bytes 589832 | tf_op jit(solution)/shard_map/ppermute | solution.py:28
  35.4 7.5 %copy-start.5 = (bf16[512,128]{1,0:T(8,128)(2,1)}, bf16[512,128]{1,0:T(8,128)(2,1)S(1)}, u32[]{:S(2)}) copy-start(bf16[512,128]{1,0:T(8,128)(2,1)S(1)} %collective-permute-done.1.refs_2_) | copy-start | bytes 393220
  35.4 19.2 %collective-permute-start.6 = (bf16[512,256]{1,0:T(8,128)(2,1)S(1)}, bf16[512,256]{1,0:T(8,128)(2,1)S(1)}, u32[]{:S(2)}, u32[]{:S(2)}) collective-permute-start(bf16[512,256]{1,0:T(8,128)(2,1)S(1)} %get-tuple-element.5), channel_id=1, source_target_pairs={{0,4},{1,5},{2,6},{3,7},{4,8},{5,9},{6,10},{7,11},{8,12},{9,13},{1... | collective-permute-start | bytes 786440 | tf_op jit(solution)/shard_map/ppermute | solution.py:28
  39.6 3.4 %copy-start.3 = (bf16[512,128]{1,0:T(8,128)(2,1)}, bf16[512,128]{1,0:T(8,128)(2,1)S(1)}, u32[]{:S(2)}) copy-start(bf16[512,128]{1,0:T(8,128)(2,1)S(1)} %collective-permute-done.2.refs_3_) | copy-start | bytes 393220
  39.6 17.9 %collective-permute-start.5 = (bf16[512,256]{1,0:T(8,128)(2,1)S(1)}, bf16[512,256]{1,0:T(8,128)(2,1)S(1)}, u32[]{:S(2)}, u32[]{:S(2)}) collective-permute-start(bf16[512,256]{1,0:T(8,128)(2,1)S(1)} %get-tuple-element.5), channel_id=1, source_target_pairs={{0,12},{1,13},{2,14},{3,15},{4,0},{5,1},{6,2},{7,3},{8,4},{9,5},{1... | collective-permute-start | bytes 786440 | tf_op jit(solution)/shard_map/ppermute | solution.py:28
  43.0 22.8 %collective-permute-start.4 = (bf16[512,512]{1,0:T(8,128)(2,1)S(1)}, bf16[512,512]{1,0:T(8,128)(2,1)S(1)}, u32[]{:S(2)}, u32[]{:S(2)}) collective-permute-start(bf16[512,512]{1,0:T(8,128)(2,1)S(1)} %constant_dynamic-update-slice_fusion), channel_id=1, source_target_pairs={{0,2},{1,3},{2,4},{3,5},{4,6},{5,7},{6,8},{7,9},{8,10},{9,11},{10,... | collective-permute-start | bytes 1572872 | tf_op jit(solution)/shard_map/ppermute | solution.py:28
  47.8 32.8 %collective-permute-start.14 = (bf16[768,384]{1,0:T(8,128)(2,1)S(1)}, bf16[768,384]{1,0:T(8,128)(2,1)S(1)}, u32[]{:S(2)}, u32[]{:S(2)}) collective-permute-start(bf16[768,384]{1,0:T(8,128)(2,1)S(1)} %constant_dynamic-update-slice_fusion.6.refs_10_), channel_id=1, source_target_pairs={{0,384},{1,385},{2,386},{3,387},{4,388},{5,389},{6,390},{7,391},{8... | collective-permute-start | bytes 1769480 | tf_op jit(solution)/shard_map/ppermute | solution.py:28
  52.2 30.4 %collective-permute-start.13 = (bf16[768,384]{1,0:T(8,128)(2,1)S(1)}, bf16[768,384]{1,0:T(8,128)(2,1)S(1)}, u32[]{:S(2)}, u32[]{:S(2)}) collective-permute-start(bf16[768,384]{1,0:T(8,128)(2,1)S(1)} %constant_dynamic-update-slice_fusion.6.refs_10_), channel_id=1, source_target_pairs={{0,256},{1,257},{2,258},{3,259},{4,260},{5,261},{6,262},{7,263},{8... | collective-permute-start | bytes 1769480 | tf_op jit(solution)/shard_map/ppermute | solution.py:28
  54.6 0.7 copy-start.11
  55.3 29.6 %collective-permute-start.12 = (bf16[768,384]{1,0:T(8,128)(2,1)S(1)}, bf16[768,384]{1,0:T(8,128)(2,1)}, u32[]{:S(2)}, u32[]{:S(2)}) collective-permute-start(bf16[768,384]{1,0:T(8,128)(2,1)S(1)} %constant_dynamic-update-slice_fusion.6.refs_10_), channel_id=1, source_target_pairs={{0,128},{1,129},{2,130},{3,131},{4,132},{5,133},{6,134},{7,135},{8... | collective-permute-start | bytes 1769480 | tf_op jit(solution)/shard_map/ppermute | solution.py:28
  57.5 0.7 copy-start.13
  58.2 17.4 %collective-permute-start.3 = (bf16[512,512]{1,0:T(8,128)(2,1)S(1)}, bf16[512,512]{1,0:T(8,128)(2,1)S(1)}, u32[]{:S(2)}, u32[]{:S(2)}) collective-permute-start(bf16[512,512]{1,0:T(8,128)(2,1)S(1)} %constant_dynamic-update-slice_fusion), channel_id=1, source_target_pairs={{0,14},{1,15},{2,0},{3,1},{4,2},{5,3},{6,4},{7,5},{8,6},{9,7},{10,... | collective-permute-start | bytes 1572872 | tf_op jit(solution)/shard_map/ppermute | solution.py:28
  65.8 0.8 copy-start.7
  66.6 20.4 %collective-permute-start.7 = (bf16[256,1536]{1,0:T(8,128)(2,1)}, bf16[256,1536]{1,0:T(8,128)(2,1)S(1)}, u32[]{:S(2)}, u32[]{:S(2)}) collective-permute-start(bf16[256,1536]{1,0:T(8,128)(2,1)} %refs_8_.1), channel_id=1, source_target_pairs={{0,16},{1,17},{2,18},{3,19},{4,20},{5,21},{6,22},{7,23},{8,24},{9,... | collective-permute-start | bytes 2359304 | tf_op jit(solution)/shard_map/ppermute | solution.py:28
  75.6 0.8 copy-start.9
  76.4 10.6 %collective-permute-start.11 = (bf16[768,384]{1,0:T(8,128)(2,1)S(1)}, bf16[768,384]{1,0:T(8,128)(2,1)}, u32[]{:S(2)}, u32[]{:S(2)}) collective-permute-start(bf16[768,384]{1,0:T(8,128)(2,1)S(1)} %constant_dynamic-update-slice_fusion.6.refs_10_), channel_id=1, source_target_pairs={{0,16},{1,17},{2,18},{3,19},{4,20},{5,21},{6,22},{7,23},{8,24},{9,... | collective-permute-start | bytes 1769480 | tf_op jit(solution)/shard_map/ppermute | solution.py:28
  80.6 6.4 %collective-permute-start.17 = (bf16[768,384]{1,0:T(8,128)(2,1)S(1)}, bf16[768,384]{1,0:T(8,128)(2,1)}, u32[]{:S(2)}, u32[]{:S(2)}) collective-permute-start(bf16[768,384]{1,0:T(8,128)(2,1)S(1)} %collective-permute-done.14.refs_14_), channel_id=1, source_target_pairs={{0,16},{1,17},{2,18},{3,19},{4,20},{5,21},{6,22},{7,23},{8,24},{9,... | collective-permute-start | bytes 1769480 | tf_op jit(solution)/shard_map/ppermute | solution.py:28
  82.5 4.5 %collective-permute-start.16 = (bf16[768,384]{1,0:T(8,128)(2,1)S(1)}, bf16[768,384]{1,0:T(8,128)(2,1)}, u32[]{:S(2)}, u32[]{:S(2)}) collective-permute-start(bf16[768,384]{1,0:T(8,128)(2,1)S(1)} %collective-permute-done.13.refs_13_), channel_id=1, source_target_pairs={{0,16},{1,17},{2,18},{3,19},{4,20},{5,21},{6,22},{7,23},{8,24},{9,... | collective-permute-start | bytes 1769480 | tf_op jit(solution)/shard_map/ppermute | solution.py:28
  84.9 4.2 %collective-permute-start.15 = (bf16[768,384]{1,0:T(8,128)(2,1)}, bf16[768,384]{1,0:T(8,128)(2,1)}, u32[]{:S(2)}, u32[]{:S(2)}) collective-permute-start(bf16[768,384]{1,0:T(8,128)(2,1)} %collective-permute-done.12.refs_12_), channel_id=1, source_target_pairs={{0,16},{1,17},{2,18},{3,19},{4,20},{5,21},{6,22},{7,23},{8,24},{9,... | collective-permute-start | bytes 1769480 | tf_op jit(solution)/shard_map/ppermute | solution.py:28
  89.2 1.9 %copy-start = (f32[512,1536]{1,0:T(8,128)S(1)}, f32[512,1536]{1,0:T(8,128)}, u32[]{:S(2)}) copy-start(f32[512,1536]{1,0:T(8,128)} %refs_18_.1) | copy-start | bytes 9437188
  91.1 0.9 copy-start.2
  92.0 0.9 copy-start.4
  92.9 0.9 copy-start.6
  93.8 1.0 copy-start.8
  94.8 1.0 copy-start.10
  95.9 0.9 copy-start.12
  96.8 0.9 copy-start.14

commit v2 on v0

v2 whole, which is shorter than its diff:
```python
import functools

import jax
import jax.numpy as jnp
from jax import lax
from jax.experimental import pallas as pl
from jax.experimental.pallas import tpu as pltpu
from jax.sharding import PartitionSpec as P

AXES = ("dp", "row", "col")
X, YL, CORES, Z, YH = 4, 4, 2, 8, 2
TOK, KB, FF = 512, 256, 1536
Q = FF // X
HALF = KB // YH


def send(array, to):
    pairs = []
    for x in range(X):
        for yl in range(YL):
            for c in range(CORES):
                for z in range(Z):
                    for yh in range(YH):
                        x2, yl2, c2, z2, yh2 = to(x, yl, c, z, yh)
                        source = (x * YL * CORES + yl * CORES + c) * Z * YH + z * YH + yh
                        target = ((x2 % X) * YL * CORES + yl2 * CORES + c2) * Z * YH + (z2 % Z) * YH + yh2
                        pairs.append((source, target))
    return lax.ppermute(array, AXES, pairs)


def swap(array):
    return send(array, lambda x, yl, c, z, yh: (x, yl, 1 - c, z, yh))


def gelu(v):
    return 0.5 * v * (1.0 + jnp.tanh(0.7978845608028654 * (v + 0.044715 * (v * v * v))))


def kernel(place, tokens, y0, y2, x1, x3, s0, s2, s1, s3, acc, out, t, w, sums, result, t_sem, w_sem, a_sem, o_sem):
    d, c = place[0], place[1]

    def start(source, target, sem):
        copy = pltpu.make_async_copy(source, target, sem)
        copy.start()
        return copy

    t_copies = []
    for z in range(Z):
        side = lax.bitwise_xor(z % CORES, c)
        at = pl.multiple_of(side * (YL * KB) + z // CORES * KB, KB)
        t_copies.append(start(tokens.at[z], t.at[:, pl.ds(at, KB)], t_sem.at[z]))
    pairs = (((y0, s0), (y2, s2)), ((x1, s1), (x3, s3)))
    w_copies, a_copies = [[], []], [[], []]
    for p in range(2):
        for i in range(2):
            j = p + 2 * i
            columns = pl.ds(i * Q, Q)
            for side in range(2):
                w_copies[p].append(start(
                    pairs[p][i][side], w.at[p, pl.ds(side * YL * KB, YL * KB), columns], w_sem.at[j * 2 + side]))
            at = pl.multiple_of(lax.bitwise_xor(d, j) * Q, 128)
            a_copies[p].append(start(acc.at[:, pl.ds(at, Q)], sums.at[p, :, columns], a_sem.at[j]))
    for copy in t_copies:
        copy.wait()
    o_copies = []
    for p in range(2):
        for copy in w_copies[p] + a_copies[p]:
            copy.wait()
        for m in range(0, TOK, 256):
            rows = slice(m, m + 256)
            total = sums[p, rows] + jnp.dot(t[rows], w[p], preferred_element_type=jnp.float32)
            result[p, rows] = gelu(total).astype(jnp.bfloat16)
        for i in range(2):
            at = pl.multiple_of(lax.bitwise_xor(d, p + 2 * i) * Q, 128)
            o_copies.append(start(
                result.at[p, :, pl.ds(i * Q, Q)], out.at[:, pl.ds(at, Q)], o_sem.at[p * 2 + i]))
    for copy in o_copies:
        copy.wait()


def along_y(block, gather):
    groups = [[yl * CORES + c for yl in range(YL)] for c in range(CORES)]
    if gather:
        return lax.all_gather(block, "row", axis=0, tiled=True, axis_index_groups=groups)
    parts = jnp.broadcast_to(block[None], (YL, *block.shape))
    return lax.all_to_all(parts, "row", 0, 0, axis_index_groups=groups).reshape(YL * block.shape[0], block.shape[1])


def along_z(parts):
    groups = [[z * YH + yh for z in range(Z)] for yh in range(YH)]
    return lax.all_to_all(parts, "col", 0, 0, axis_index_groups=groups)


def after(value, *others):
    return lax.optimization_barrier((value, *others))[0]


def shards(t, w, acc):
    d, r, col = lax.axis_index("dp"), lax.axis_index("row"), lax.axis_index("col")
    yh = col % YH
    place = jnp.stack([d, r % CORES]).astype(jnp.int32)

    def quarter(j):
        return lax.dynamic_slice(w, (0, lax.bitwise_xor(d, j) * Q), (KB, Q))

    t1 = send(t, lambda x, yl, c, z, yh: (x, yl, c, z, 1 - yh))
    t0 = jnp.where(yh == 0, jnp.concatenate([t, t1], axis=1), jnp.concatenate([t1, t], axis=1))
    parts = jnp.broadcast_to(t0[None], (Z, *t0.shape))
    tokens = along_z(parts)
    y0 = along_y(quarter(0), True)
    x1 = send(y0, lambda x, yl, c, z, yh: (x ^ 1, yl, c, z, yh))
    x3 = send(y0, lambda x, yl, c, z, yh: (x ^ 3, yl, c, z, yh))
    y2 = along_y(after(quarter(2), y0), True)
    s0, s2, s1, s3 = (swap(a) for a in (y0, y2, x1, x3))

    return pl.pallas_call(
        kernel,
        out_shape=jax.ShapeDtypeStruct((TOK, FF), jnp.bfloat16),
        in_specs=[pl.BlockSpec(memory_space=pltpu.SMEM)] + [pl.BlockSpec(memory_space=pl.ANY)] * 10,
        out_specs=pl.BlockSpec(memory_space=pl.ANY),
        scratch_shapes=[
            pltpu.VMEM((TOK, Z * KB), jnp.bfloat16),
            pltpu.VMEM((2, Z * KB, 2 * Q), jnp.bfloat16),
            pltpu.VMEM((2, TOK, 2 * Q), jnp.float32),
            pltpu.VMEM((2, TOK, 2 * Q), jnp.bfloat16),
            pltpu.SemaphoreType.DMA((Z,)),
            pltpu.SemaphoreType.DMA((8,)),
            pltpu.SemaphoreType.DMA((4,)),
            pltpu.SemaphoreType.DMA((4,)),
        ],
        compiler_params=pltpu.CompilerParams(vmem_limit_bytes=56 * 1024 * 1024),
        cost_estimate=pl.CostEstimate(
            flops=2 * TOK * FF * Z * KB, bytes_accessed=13 * 1024 * 1024, transcendentals=TOK * FF
        ),
    )(place, tokens, y0, y2, x1, x3, s0, s2, s1, s3, acc)


def solution(mesh):
    return jax.shard_map(
        shards,
        mesh=mesh,
        in_specs=(P(("dp", "row"), "col"), P("row", "col"), P(("dp", "row"), "col")),
        out_specs=P(("dp", "row"), "col"),
        check_vma=False,
    )
```

time: 210 us -> 95.5 us (0.45)
  waiting for transfers between devices: 186 us -> 6.73 us
  starting transfers between devices: 0.04 us -> 38.4 us
  blocking collectives: 0 us -> 35.7 us
  between operations: 13.4 us -> 0.12 us
  Pallas kernels: 0 us -> 9.61 us
  matrix products: 9.43 us -> 0 us
  local copies, waits for them, and re-layouts: 0 us -> 2.85 us
    all_gather x2 -> x0, waiting for transfers between devices: 184 us -> none  [the longest x1 106 us: shards(): lax.all_gather(tokens_window, 'col', axis=1, tiled=True)]
    all_gather x0 -> x2, blocking collectives: none -> 35.7 us  [along_y(): lax.all_gather(block, 'row', axis=0, tiled=True, axis_index_groups=groups)]
    ppermute x0 -> x7, starting transfers between devices: none -> 30.1 us  [send(): return lax.ppermute(array, AXES, pairs)]
    pallas_call x0 -> x1, Pallas kernels: none -> 9.61 us  [shards(): pl.pallas_call(kernel, out_shape=jax.ShapeDtypeStruct((TOK, FF), jnp.bflo...]
    dot_general x1 -> x0, matrix products: 9.43 us -> none  [shards(): jnp.dot(lax.all_gather(tokens_window, 'col', axis=1, tiled=True), weight_...]
    all_to_all x0 -> x1, starting transfers between devices: none -> 8.3 us  [along_z(): return lax.all_to_all(parts, 'col', 0, 0, axis_index_groups=groups)]
    ppermute x0 -> x7, waiting for transfers between devices: none -> 6.73 us  [send(): return lax.ppermute(array, AXES, pairs)]
  transfers between devices with their start and end apart: 2 -> 8, of which waited for: 2 -> 2; matrix products, arithmetic and copies ran while one was open for 0% -> 1% of each run, Pallas kernels for 0% -> 0%
where the time goes in v2:
time: 95.5 us; the launch traced here: 95.1 us
  starting transfers between devices  38.4 us (40%)
  blocking collectives  35.7 us (37%)
  Pallas kernels  9.61 us (10%)
  waiting for transfers between devices  6.73 us (7%)
  local copies, waits for them, and re-layouts  2.85 us (3%)
  other arithmetic  1.72 us (2%)
    all_gather x2, blocking collectives, along_y(): lax.all_gather(block, 'row', axis=0, tiled=True, axis_index_groups=groups)  35.7 us
    ppermute x7, starting transfers between devices, send(): return lax.ppermute(array, AXES, pairs)  30.1 us
    pallas_call x1, Pallas kernels, shards(): pl.pallas_call(kernel, out_shape=jax.ShapeDtypeStruct((TOK, FF), jnp.bflo...  9.61 us
    all_to_all x1, starting transfers between devices, along_z(): return lax.all_to_all(parts, 'col', 0, 0, axis_index_groups=groups)  8.3 us
    ppermute x7, waiting for transfers between devices, send(): return lax.ppermute(array, AXES, pairs)  6.73 us
  transfers between devices with their start and end apart: 8, of which 2 were waited for; matrix products, arithmetic and copies ran while one was open for 1% of the time, Pallas kernels for 0%

profile of v2, /device:TPU:1, one launch (start us, length us, event | category | flops | bytes accessed | tf_op | source)
XLA Modules:
  0.0 95.1 jit_solution(10957985751892661997)
XLA Ops:
  0.0 8.3 %collective-permute-start = (bf16[512,128]{1,0:T(8,128)(2,1)}, bf16[512,128]{1,0:T(8,128)(2,1)S(1)}, u32[]{:S(2)}, u32[]{:S(2)}) collective-permute-start(bf16[512,128]{1,0:T(8,128)(2,1)} %param.3), channel_id=1, source_target_pairs={{0,1},{1,0},{2,3},{3,2},{4,5},{5,4},{6,7},{7,6},{8,9},{9,8},{10,11... | collective-permute-start | bytes 393224 | tf_op jit(solution)/shard_map/ppermute | solution.py:28
  8.3 5.2 %collective-permute-done = bf16[512,128]{1,0:T(8,128)(2,1)S(1)} collective-permute-done((bf16[512,128]{1,0:T(8,128)(2,1)}, bf16[512,128]{1,0:T(8,128)(2,1)S(1)}, u32[]{:S(2)}, u32[]{:S(2)}) %collective-permute-start) | collective-permute-done | bytes 131104 | tf_op jit(solution)/shard_map/ppermute | solution.py:28
  13.5 1.1 %maximum_select_fusion = bf16[512,256]{1,0:T(8,128)(2,1)S(1)} fusion(bf16[512,128]{1,0:T(8,128)(2,1)S(1)} %collective-permute-done, bf16[512,128]{1,0:T(8,128)(2,1)} %param.3, pred[]{:T(512)S(6)} %eq.6), kind=kLoop, calls=%fused_computation | loop fusion | flops 1179648 | bytes 524289 | tf_op jit(solution)/shard_map/jit(_where)/select_n | solution.py:107
  14.5 1.5 %broadcast_in_dim.2 = bf16[8,512,256]{2,1,0:T(8,128)(2,1)} broadcast(bf16[512,256]{1,0:T(8,128)(2,1)S(1)} %maximum_select_fusion), dimensions={1,2} | broadcast | bytes 2359296 | tf_op jit(solution)/shard_map/broadcast_in_dim | solution.py:108
  16.0 0.0 copy-start.2
  16.0 8.3 %all-to-all-start = ((bf16[8,512,256]{2,1,0:T(8,128)(2,1)}), bf16[8,512,256]{2,1,0:T(8,128)(2,1)S(1)}, u32[]{:S(2)}, u32[]{:S(2)}) async-start(bf16[8,512,256]{2,1,0:T(8,128)(2,1)} %broadcast_in_dim.2), calls=%async_computation | async-start | bytes 4194304 | tf_op jit(solution)/shard_map/all_to_all | solution.py:91
  24.3 0.0 copy-done.2
  24.3 19.3 %all_gather.6.y0 = bf16[1024,384]{1,0:T(8,128)(2,1)S(1)} all-gather(bf16[256,384]{1,0:T(8,128)(2,1)S(1)} %get-tuple-element.8), channel_id=1, replica_groups={{0,32,64,96},{16,48,80,112},{1,33,65,97},{17,49,81,113},{2,34,66,98},{1..., dimensions={0}, use_global_device_ids=true | all-gather | bytes 983040 | tf_op jit(solution)/shard_map/all_gather | solution.py:84
  43.6 0.0 copy-start.1
  43.6 3.1 %collective-permute-start.1 = (bf16[1024,384]{1,0:T(8,128)(2,1)S(1)}, bf16[1024,384]{1,0:T(8,128)(2,1)}, u32[]{:S(2)}, u32[]{:S(2)}) collective-permute-start(bf16[1024,384]{1,0:T(8,128)(2,1)S(1)} %all_gather.6.y0), channel_id=1, source_target_pairs={{0,128},{1,129},{2,130},{3,131},{4,132},{5,133},{6,134},{7,135},{8... | collective-permute-start | bytes 2359304 | tf_op jit(solution)/shard_map/ppermute | solution.py:28
  46.8 3.7 %collective-permute-start.2 = (bf16[1024,384]{1,0:T(8,128)(2,1)S(1)}, bf16[1024,384]{1,0:T(8,128)(2,1)}, u32[]{:S(2)}, u32[]{:S(2)}) collective-permute-start(bf16[1024,384]{1,0:T(8,128)(2,1)S(1)} %all_gather.6.y0), channel_id=1, source_target_pairs={{0,384},{1,385},{2,386},{3,387},{4,388},{5,389},{6,390},{7,391},{8... | collective-permute-start | bytes 2359304 | tf_op jit(solution)/shard_map/ppermute | solution.py:28
  50.5 6.5 %collective-permute-start.3 = (bf16[1024,384]{1,0:T(8,128)(2,1)S(1)}, bf16[1024,384]{1,0:T(8,128)(2,1)}, u32[]{:S(2)}, u32[]{:S(2)}) collective-permute-start(bf16[1024,384]{1,0:T(8,128)(2,1)S(1)} %all_gather.6.y0), channel_id=1, source_target_pairs={{0,16},{1,17},{2,18},{3,19},{4,20},{5,21},{6,22},{7,23},{8,24},{9,... | collective-permute-start | bytes 2359304 | tf_op jit(solution)/shard_map/ppermute | solution.py:28
  57.0 16.4 %all_gather.7.y2 = bf16[1024,384]{1,0:T(8,128)(2,1)} all-gather(bf16[256,384]{1,0:T(8,128)(2,1)S(1)} %get-tuple-element.6), channel_id=1, replica_groups={{0,32,64,96},{16,48,80,112},{1,33,65,97},{17,49,81,113},{2,34,66,98},{1..., dimensions={0}, use_global_device_ids=true | all-gather | bytes 983040 | tf_op jit(solution)/shard_map/all_gather | solution.py:84
  73.4 4.2 %collective-permute-start.4 = (bf16[1024,384]{1,0:T(8,128)(2,1)}, bf16[1024,384]{1,0:T(8,128)(2,1)}, u32[]{:S(2)}, u32[]{:S(2)}) collective-permute-start(bf16[1024,384]{1,0:T(8,128)(2,1)} %all_gather.7.y2), channel_id=1, source_target_pairs={{0,16},{1,17},{2,18},{3,19},{4,20},{5,21},{6,22},{7,23},{8,24},{9,... | collective-permute-start | bytes 2359304 | tf_op jit(solution)/shard_map/ppermute | solution.py:28
  77.6 0.0 collective-permute-done.1.x1
  77.6 1.9 %collective-permute-start.5 = (bf16[1024,384]{1,0:T(8,128)(2,1)}, bf16[1024,384]{1,0:T(8,128)(2,1)}, u32[]{:S(2)}, u32[]{:S(2)}) collective-permute-start(bf16[1024,384]{1,0:T(8,128)(2,1)} %collective-permute-done.1.x1), channel_id=1, source_target_pairs={{0,16},{1,17},{2,18},{3,19},{4,20},{5,21},{6,22},{7,23},{8,24},{9,... | collective-permute-start | bytes 2359304 | tf_op jit(solution)/shard_map/ppermute | solution.py:28
  79.5 0.0 collective-permute-done.2.x3
  79.5 2.4 %collective-permute-start.6 = (bf16[1024,384]{1,0:T(8,128)(2,1)}, bf16[1024,384]{1,0:T(8,128)(2,1)}, u32[]{:S(2)}, u32[]{:S(2)}) collective-permute-start(bf16[1024,384]{1,0:T(8,128)(2,1)} %collective-permute-done.2.x3), channel_id=1, source_target_pairs={{0,16},{1,17},{2,18},{3,19},{4,20},{5,21},{6,22},{7,23},{8,24},{9,... | collective-permute-start | bytes 2359304 | tf_op jit(solution)/shard_map/ppermute | solution.py:28
  82.0 0.7 pad_add_fusion.place
  82.6 0.0 collective-permute-done.4.s2
  82.6 0.0 collective-permute-done.3.s0
  82.6 0.0 collective-permute-done.5.s1
  82.6 1.5 %collective-permute-done.6.s3 = bf16[1024,384]{1,0:T(8,128)(2,1)} collective-permute-done((bf16[1024,384]{1,0:T(8,128)(2,1)}, bf16[1024,384]{1,0:T(8,128)(2,1)}, u32[]{:S(2)}, u32[]{:S(2)}) %collective-permute-start.6) | collective-permute-done | bytes 786464 | tf_op jit(solution)/shard_map/ppermute | solution.py:28
  84.2 0.0 all-to-all-done.tokens
  84.2 0.0 copy-done.1
  84.2 0.0 copy-start
  84.2 1.3 %copy-done = bf16[8,512,256]{2,1,0:T(8,128)(2,1)} copy-done((bf16[8,512,256]{2,1,0:T(8,128)(2,1)}, bf16[8,512,256]{2,1,0:T(8,128)(2,1)S(1)}, u32[]{:S(2)}) %copy-start) | copy-done | bytes 2097176
  85.5 9.6 %shard_map.37 = bf16[512,1536]{1,0:T(8,128)(2,1)} custom-call(s32[2]{0:T(128)} %pad_add_fusion.place, bf16[8,512,256]{2,1,0:T(8,128)(2,1)} %copy-done, bf16[1024,384]{1,0:T(8,128)(2,1)} %copy-done.1, bf16[1024,384]{1,0:T(8,128)(2,1)} %all_gather.7.y2, bf16[1024,384]{1,0:T(8,128)(2,1)} %collective-permute-done.1.x1, ...), custom_call_target="tpu_custom_call" | custom-call | flops 3221225472 | bytes 13631488 | tf_op jit(solution)/shard_map/pallas_call | solution.py:116
  (1 shorter events, 0.0 us)
Async XLA Ops:
  0.0 13.5 %collective-permute-start = (bf16[512,128]{1,0:T(8,128)(2,1)}, bf16[512,128]{1,0:T(8,128)(2,1)S(1)}, u32[]{:S(2)}, u32[]{:S(2)}) collective-permute-start(bf16[512,128]{1,0:T(8,128)(2,1)} %param.3), channel_id=1, source_target_pairs={{0,1},{1,0},{2,3},{3,2},{4,5},{5,4},{6,7},{7,6},{8,9},{9,8},{10,11... | collective-permute-start | bytes 393224 | tf_op jit(solution)/shard_map/ppermute | solution.py:28
  16.0 8.3 %copy-start.2 = (bf16[256,1536]{1,0:T(8,128)(2,1)S(1)}, bf16[256,1536]{1,0:T(8,128)(2,1)}, u32[]{:S(2)}) copy-start(bf16[256,1536]{1,0:T(8,128)(2,1)} %param.4) | copy-start | bytes 2359300
  16.0 68.2 %all-to-all-start = ((bf16[8,512,256]{2,1,0:T(8,128)(2,1)}), bf16[8,512,256]{2,1,0:T(8,128)(2,1)S(1)}, u32[]{:S(2)}, u32[]{:S(2)}) async-start(bf16[8,512,256]{2,1,0:T(8,128)(2,1)} %broadcast_in_dim.2), calls=%async_computation | async-start | bytes 4194304 | tf_op jit(solution)/shard_map/all_to_all | solution.py:91
  43.6 40.6 %copy-start.1 = (bf16[1024,384]{1,0:T(8,128)(2,1)}, bf16[1024,384]{1,0:T(8,128)(2,1)S(1)}, u32[]{:S(2)}) copy-start(bf16[1024,384]{1,0:T(8,128)(2,1)S(1)} %all_gather.6.y0) | copy-start | bytes 2359300
  43.6 34.0 %collective-permute-start.1 = (bf16[1024,384]{1,0:T(8,128)(2,1)S(1)}, bf16[1024,384]{1,0:T(8,128)(2,1)}, u32[]{:S(2)}, u32[]{:S(2)}) collective-permute-start(bf16[1024,384]{1,0:T(8,128)(2,1)S(1)} %all_gather.6.y0), channel_id=1, source_target_pairs={{0,128},{1,129},{2,130},{3,131},{4,132},{5,133},{6,134},{7,135},{8... | collective-permute-start | bytes 2359304 | tf_op jit(solution)/shard_map/ppermute | solution.py:28
  46.8 32.8 %collective-permute-start.2 = (bf16[1024,384]{1,0:T(8,128)(2,1)S(1)}, bf16[1024,384]{1,0:T(8,128)(2,1)}, u32[]{:S(2)}, u32[]{:S(2)}) collective-permute-start(bf16[1024,384]{1,0:T(8,128)(2,1)S(1)} %all_gather.6.y0), channel_id=1, source_target_pairs={{0,384},{1,385},{2,386},{3,387},{4,388},{5,389},{6,390},{7,391},{8... | collective-permute-start | bytes 2359304 | tf_op jit(solution)/shard_map/ppermute | solution.py:28
  50.5 32.2 %collective-permute-start.3 = (bf16[1024,384]{1,0:T(8,128)(2,1)S(1)}, bf16[1024,384]{1,0:T(8,128)(2,1)}, u32[]{:S(2)}, u32[]{:S(2)}) collective-permute-start(bf16[1024,384]{1,0:T(8,128)(2,1)S(1)} %all_gather.6.y0), channel_id=1, source_target_pairs={{0,16},{1,17},{2,18},{3,19},{4,20},{5,21},{6,22},{7,23},{8,24},{9,... | collective-permute-start | bytes 2359304 | tf_op jit(solution)/shard_map/ppermute | solution.py:28
  73.4 9.2 %collective-permute-start.4 = (bf16[1024,384]{1,0:T(8,128)(2,1)}, bf16[1024,384]{1,0:T(8,128)(2,1)}, u32[]{:S(2)}, u32[]{:S(2)}) collective-permute-start(bf16[1024,384]{1,0:T(8,128)(2,1)} %all_gather.7.y2), channel_id=1, source_target_pairs={{0,16},{1,17},{2,18},{3,19},{4,20},{5,21},{6,22},{7,23},{8,24},{9,... | collective-permute-start | bytes 2359304 | tf_op jit(solution)/shard_map/ppermute | solution.py:28
  77.6 5.0 %collective-permute-start.5 = (bf16[1024,384]{1,0:T(8,128)(2,1)}, bf16[1024,384]{1,0:T(8,128)(2,1)}, u32[]{:S(2)}, u32[]{:S(2)}) collective-permute-start(bf16[1024,384]{1,0:T(8,128)(2,1)} %collective-permute-done.1.x1), channel_id=1, source_target_pairs={{0,16},{1,17},{2,18},{3,19},{4,20},{5,21},{6,22},{7,23},{8,24},{9,... | collective-permute-start | bytes 2359304 | tf_op jit(solution)/shard_map/ppermute | solution.py:28
  79.5 4.6 %collective-permute-start.6 = (bf16[1024,384]{1,0:T(8,128)(2,1)}, bf16[1024,384]{1,0:T(8,128)(2,1)}, u32[]{:S(2)}, u32[]{:S(2)}) collective-permute-start(bf16[1024,384]{1,0:T(8,128)(2,1)} %collective-permute-done.2.x3), channel_id=1, source_target_pairs={{0,16},{1,17},{2,18},{3,19},{4,20},{5,21},{6,22},{7,23},{8,24},{9,... | collective-permute-start | bytes 2359304 | tf_op jit(solution)/shard_map/ppermute | solution.py:28
  84.2 1.3 %copy-start = (bf16[8,512,256]{2,1,0:T(8,128)(2,1)}, bf16[8,512,256]{2,1,0:T(8,128)(2,1)S(1)}, u32[]{:S(2)}) copy-start(bf16[8,512,256]{2,1,0:T(8,128)(2,1)S(1)} %all-to-all-done.tokens) | copy-start | bytes 6291460

commit v3 on v2

--- a/solution.py
+++ b/solution.py
@@ -36,46 +36,47 @@
     return 0.5 * v * (1.0 + jnp.tanh(0.7978845608028654 * (v + 0.044715 * (v * v * v))))
 
 
-def kernel(place, tokens, y0, y2, x1, x3, s0, s2, s1, s3, acc, out, t, w, sums, result, t_sem, w_sem, a_sem, o_sem):
+def kernel(place, tokens, y0, y2, x1, x3, s0, s2, s1, s3, acc, out, w, sums, result, w_sem, a_sem, o_sem):
     d, c = place[0], place[1]
+    deep = YL * KB
 
     def start(source, target, sem):
         copy = pltpu.make_async_copy(source, target, sem)
         copy.start()
         return copy
 
-    t_copies = []
-    for z in range(Z):
-        side = lax.bitwise_xor(z % CORES, c)
-        at = pl.multiple_of(side * (YL * KB) + z // CORES * KB, KB)
-        t_copies.append(start(tokens.at[z], t.at[:, pl.ds(at, KB)], t_sem.at[z]))
+    def wait(copies):
+        for copy in copies:
+            copy.wait()
+
     pairs = (((y0, s0), (y2, s2)), ((x1, s1), (x3, s3)))
-    w_copies, a_copies = [[], []], [[], []]
+    w_copies, a_copies = [], []
     for p in range(2):
-        for i in range(2):
-            j = p + 2 * i
-            columns = pl.ds(i * Q, Q)
-            for side in range(2):
-                w_copies[p].append(start(
-                    pairs[p][i][side], w.at[p, pl.ds(side * YL * KB, YL * KB), columns], w_sem.at[j * 2 + side]))
-            at = pl.multiple_of(lax.bitwise_xor(d, j) * Q, 128)
-            a_copies[p].append(start(acc.at[:, pl.ds(at, Q)], sums.at[p, :, columns], a_sem.at[j]))
-    for copy in t_copies:
-        copy.wait()
+        w_copies.append([
+            start(pairs[p][i][side], w.at[p, pl.ds(side * deep, deep), pl.ds(i * Q, Q)], w_sem.at[p * 4 + side * 2 + i])
+            for side in range(2) for i in range(2)])
+        a_copies.append([
+            start(acc.at[:, pl.ds(pl.multiple_of(lax.bitwise_xor(d, p + 2 * i) * Q, 128), Q)],
+                  sums.at[p, :, pl.ds(i * Q, Q)], a_sem.at[p * 2 + i])
+            for i in range(2)])
     o_copies = []
     for p in range(2):
-        for copy in w_copies[p] + a_copies[p]:
-            copy.wait()
+        wait(w_copies[p])
+        wait(a_copies[p])
         for m in range(0, TOK, 256):
             rows = slice(m, m + 256)
-            total = sums[p, rows] + jnp.dot(t[rows], w[p], preferred_element_type=jnp.float32)
+            total = sums[p, rows]
+            for side in range(2):
+                for k in range(YL):
+                    block = w[p, side * deep + k * KB:side * deep + (k + 1) * KB]
+                    total += jnp.dot(
+                        tokens[k * CORES + lax.bitwise_xor(side, c), rows], block, preferred_element_type=jnp.float32)
             result[p, rows] = gelu(total).astype(jnp.bfloat16)
         for i in range(2):
             at = pl.multiple_of(lax.bitwise_xor(d, p + 2 * i) * Q, 128)
             o_copies.append(start(
                 result.at[p, :, pl.ds(i * Q, Q)], out.at[:, pl.ds(at, Q)], o_sem.at[p * 2 + i]))
-    for copy in o_copies:
-        copy.wait()
+    wait(o_copies)
 
 
 def along_y(block, gather):
@@ -111,24 +112,23 @@
     x1 = send(y0, lambda x, yl, c, z, yh: (x ^ 1, yl, c, z, yh))
     x3 = send(y0, lambda x, yl, c, z, yh: (x ^ 3, yl, c, z, yh))
     y2 = along_y(after(quarter(2), y0), True)
-    s0, s2, s1, s3 = (swap(a) for a in (y0, y2, x1, x3))
+    s0, s2, s1, s3 = (swap(a) for a in (after(y0, y2), y2, x1, x3))
 
     return pl.pallas_call(
         kernel,
         out_shape=jax.ShapeDtypeStruct((TOK, FF), jnp.bfloat16),
-        in_specs=[pl.BlockSpec(memory_space=pltpu.SMEM)] + [pl.BlockSpec(memory_space=pl.ANY)] * 10,
+        in_specs=[pl.BlockSpec(memory_space=pltpu.SMEM), pl.BlockSpec(memory_space=pltpu.VMEM)]
+        + [pl.BlockSpec(memory_space=pl.ANY)] * 9,
         out_specs=pl.BlockSpec(memory_space=pl.ANY),
         scratch_shapes=[
-            pltpu.VMEM((TOK, Z * KB), jnp.bfloat16),
             pltpu.VMEM((2, Z * KB, 2 * Q), jnp.bfloat16),
             pltpu.VMEM((2, TOK, 2 * Q), jnp.float32),
             pltpu.VMEM((2, TOK, 2 * Q), jnp.bfloat16),
-            pltpu.SemaphoreType.DMA((Z,)),
             pltpu.SemaphoreType.DMA((8,)),
             pltpu.SemaphoreType.DMA((4,)),
             pltpu.SemaphoreType.DMA((4,)),
         ],
-        compiler_params=pltpu.CompilerParams(vmem_limit_bytes=56 * 1024 * 1024),
+        compiler_params=pltpu.CompilerParams(vmem_limit_bytes=44 * 1024 * 1024),
         cost_estimate=pl.CostEstimate(
             flops=2 * TOK * FF * Z * KB, bytes_accessed=13 * 1024 * 1024, transcendentals=TOK * FF
         ),

time: 95.5 us -> 92.6 us (0.970)
  Pallas kernels: 9.61 us -> 8.22 us
  local copies, waits for them, and re-layouts: 2.85 us -> 1.52 us
    pallas_call x1, Pallas kernels: 9.61 us -> 8.22 us  [shards(): pl.pallas_call(kernel, out_shape=jax.ShapeDtypeStruct((TOK, FF), jnp.bflo...]
    unnamed x6 -> x2, local copies, waits for them, and re-layouts: 1.34 us -> 0.01 us
  transfers between devices with their start and end apart: 8 -> 8, of which waited for: 2 -> 3; matrix products, arithmetic and copies ran while one was open for 1% -> 0% of each run, Pallas kernels for 0% -> 0%
where the time goes in v3:
time: 92.6 us; the launch traced here: 92.2 us
  starting transfers between devices  38 us (41%)
  blocking collectives  35.6 us (38%)
  Pallas kernels  8.22 us (9%)
  waiting for transfers between devices  7.68 us (8%)
  local copies, waits for them, and re-layouts  1.52 us (2%)
  other arithmetic  1.13 us (1%)
    all_gather x2, blocking collectives, along_y(): lax.all_gather(block, 'row', axis=0, tiled=True, axis_index_groups=groups)  35.6 us
    ppermute x7, starting transfers between devices, send(): return lax.ppermute(array, AXES, pairs)  29.7 us
    all_to_all x1, starting transfers between devices, along_z(): return lax.all_to_all(parts, 'col', 0, 0, axis_index_groups=groups)  8.3 us
    pallas_call x1, Pallas kernels, shards(): pl.pallas_call(kernel, out_shape=jax.ShapeDtypeStruct((TOK, FF), jnp.bflo...  8.22 us
    ppermute x7, waiting for transfers between devices, send(): return lax.ppermute(array, AXES, pairs)  7.68 us
  transfers between devices with their start and end apart: 8, of which 3 were waited for; matrix products, arithmetic and copies ran while one was open for 0% of the time, Pallas kernels for 0%

profile of v3, /device:TPU:1, one launch (start us, length us, event | category | flops | bytes accessed | tf_op | source)
XLA Modules:
  0.0 92.2 jit_solution(655831382524407668)
XLA Ops:
  0.0 8.3 %collective-permute-start = (bf16[512,128]{1,0:T(8,128)(2,1)}, bf16[512,128]{1,0:T(8,128)(2,1)S(1)}, u32[]{:S(2)}, u32[]{:S(2)}) collective-permute-start(bf16[512,128]{1,0:T(8,128)(2,1)} %param.3), channel_id=1, source_target_pairs={{0,1},{1,0},{2,3},{3,2},{4,5},{5,4},{6,7},{7,6},{8,9},{9,8},{10,11... | collective-permute-start | bytes 393224 | tf_op jit(solution)/shard_map/ppermute | solution.py:28
  8.3 5.2 %collective-permute-done = bf16[512,128]{1,0:T(8,128)(2,1)S(1)} collective-permute-done((bf16[512,128]{1,0:T(8,128)(2,1)}, bf16[512,128]{1,0:T(8,128)(2,1)S(1)}, u32[]{:S(2)}, u32[]{:S(2)}) %collective-permute-start) | collective-permute-done | bytes 131104 | tf_op jit(solution)/shard_map/ppermute | solution.py:28
  13.5 1.1 %maximum_select_fusion = bf16[512,256]{1,0:T(8,128)(2,1)S(1)} fusion(bf16[512,128]{1,0:T(8,128)(2,1)S(1)} %collective-permute-done, bf16[512,128]{1,0:T(8,128)(2,1)} %param.3, pred[]{:T(512)S(6)} %eq.6), kind=kLoop, calls=%fused_computation | loop fusion | flops 1179648 | bytes 524289 | tf_op jit(solution)/shard_map/jit(_where)/select_n | solution.py:108
  14.5 1.5 %broadcast_in_dim.2 = bf16[8,512,256]{2,1,0:T(8,128)(2,1)} broadcast(bf16[512,256]{1,0:T(8,128)(2,1)S(1)} %maximum_select_fusion), dimensions={1,2} | broadcast | bytes 2359296 | tf_op jit(solution)/shard_map/broadcast_in_dim | solution.py:109
  16.0 0.0 copy-start
  16.0 8.3 %all-to-all-start = ((bf16[8,512,256]{2,1,0:T(8,128)(2,1)}), bf16[8,512,256]{2,1,0:T(8,128)(2,1)S(1)}, u32[]{:S(2)}, u32[]{:S(2)}) async-start(bf16[8,512,256]{2,1,0:T(8,128)(2,1)} %broadcast_in_dim.2), calls=%async_computation | async-start | bytes 4194304 | tf_op jit(solution)/shard_map/all_to_all | solution.py:92
  24.3 0.0 copy-done
  24.3 19.3 %all_gather.6.y0 = bf16[1024,384]{1,0:T(8,128)(2,1)S(1)} all-gather(bf16[256,384]{1,0:T(8,128)(2,1)S(1)} %get-tuple-element.10), channel_id=1, replica_groups={{0,32,64,96},{16,48,80,112},{1,33,65,97},{17,49,81,113},{2,34,66,98},{1..., dimensions={0}, use_global_device_ids=true | all-gather | bytes 983040 | tf_op jit(solution)/shard_map/all_gather | solution.py:85
  43.6 3.1 %collective-permute-start.1 = (bf16[1024,384]{1,0:T(8,128)(2,1)S(1)}, bf16[1024,384]{1,0:T(8,128)(2,1)}, u32[]{:S(2)}, u32[]{:S(2)}) collective-permute-start(bf16[1024,384]{1,0:T(8,128)(2,1)S(1)} %all_gather.6.y0), channel_id=1, source_target_pairs={{0,128},{1,129},{2,130},{3,131},{4,132},{5,133},{6,134},{7,135},{8... | collective-permute-start | bytes 2359304 | tf_op jit(solution)/shard_map/ppermute | solution.py:28
  46.8 3.7 %collective-permute-start.2 = (bf16[1024,384]{1,0:T(8,128)(2,1)S(1)}, bf16[1024,384]{1,0:T(8,128)(2,1)}, u32[]{:S(2)}, u32[]{:S(2)}) collective-permute-start(bf16[1024,384]{1,0:T(8,128)(2,1)S(1)} %all_gather.6.y0), channel_id=1, source_target_pairs={{0,384},{1,385},{2,386},{3,387},{4,388},{5,389},{6,390},{7,391},{8... | collective-permute-start | bytes 2359304 | tf_op jit(solution)/shard_map/ppermute | solution.py:28
  50.5 16.3 %all_gather.7.y2 = bf16[1024,384]{1,0:T(8,128)(2,1)} all-gather(bf16[256,384]{1,0:T(8,128)(2,1)S(1)} %get-tuple-element.7), channel_id=1, replica_groups={{0,32,64,96},{16,48,80,112},{1,33,65,97},{17,49,81,113},{2,34,66,98},{1..., dimensions={0}, use_global_device_ids=true | all-gather | bytes 983040 | tf_op jit(solution)/shard_map/all_gather | solution.py:85
  66.8 8.3 %collective-permute-start.4 = (bf16[1024,384]{1,0:T(8,128)(2,1)}, bf16[1024,384]{1,0:T(8,128)(2,1)}, u32[]{:S(2)}, u32[]{:S(2)}) collective-permute-start(bf16[1024,384]{1,0:T(8,128)(2,1)} %all_gather.7.y2), channel_id=1, source_target_pairs={{0,16},{1,17},{2,18},{3,19},{4,20},{5,21},{6,22},{7,23},{8,24},{9,... | collective-permute-start | bytes 2359304 | tf_op jit(solution)/shard_map/ppermute | solution.py:28
  75.1 1.9 %collective-permute-start.3 = (bf16[1024,384]{1,0:T(8,128)(2,1)S(1)}, bf16[1024,384]{1,0:T(8,128)(2,1)}, u32[]{:S(2)}, u32[]{:S(2)}) collective-permute-start(bf16[1024,384]{1,0:T(8,128)(2,1)S(1)} %all_gather.6.y0), channel_id=1, source_target_pairs={{0,16},{1,17},{2,18},{3,19},{4,20},{5,21},{6,22},{7,23},{8,24},{9,... | collective-permute-start | bytes 2359304 | tf_op jit(solution)/shard_map/ppermute | solution.py:28
  77.1 0.0 collective-permute-done.1.x1
  77.1 2.4 %collective-permute-start.5 = (bf16[1024,384]{1,0:T(8,128)(2,1)}, bf16[1024,384]{1,0:T(8,128)(2,1)}, u32[]{:S(2)}, u32[]{:S(2)}) collective-permute-start(bf16[1024,384]{1,0:T(8,128)(2,1)} %collective-permute-done.1.x1), channel_id=1, source_target_pairs={{0,16},{1,17},{2,18},{3,19},{4,20},{5,21},{6,22},{7,23},{8,24},{9,... | collective-permute-start | bytes 2359304 | tf_op jit(solution)/shard_map/ppermute | solution.py:28
  79.5 0.0 collective-permute-done.2.x3
  79.5 1.9 %collective-permute-start.6 = (bf16[1024,384]{1,0:T(8,128)(2,1)}, bf16[1024,384]{1,0:T(8,128)(2,1)}, u32[]{:S(2)}, u32[]{:S(2)}) collective-permute-start(bf16[1024,384]{1,0:T(8,128)(2,1)} %collective-permute-done.2.x3), channel_id=1, source_target_pairs={{0,16},{1,17},{2,18},{3,19},{4,20},{5,21},{6,22},{7,23},{8,24},{9,... | collective-permute-start | bytes 2359304 | tf_op jit(solution)/shard_map/ppermute | solution.py:28
  81.4 0.1 pad_add_fusion.place
  81.5 0.0 collective-permute-done.3.s0
  81.5 0.0 collective-permute-done.4.s2
  81.5 0.2 collective-permute-done.5.s1
  81.7 2.3 %collective-permute-done.6.s3 = bf16[1024,384]{1,0:T(8,128)(2,1)} collective-permute-done((bf16[1024,384]{1,0:T(8,128)(2,1)}, bf16[1024,384]{1,0:T(8,128)(2,1)}, u32[]{:S(2)}, u32[]{:S(2)}) %collective-permute-start.6) | collective-permute-done | bytes 786464 | tf_op jit(solution)/shard_map/ppermute | solution.py:28
  84.0 0.0 all-to-all-done.tokens
  84.0 8.2 %shard_map.37 = bf16[512,1536]{1,0:T(8,128)(2,1)} custom-call(s32[2]{0:T(128)S(1)} %pad_add_fusion.place, bf16[8,512,256]{2,1,0:T(8,128)(2,1)S(1)} %all-to-all-done.tokens, bf16[1024,384]{1,0:T(8,128)(2,1)S(1)} %all_gather.6.y0, bf16[1024,384]{1,0:T(8,128)(2,1)} %all_gather.7.y2, bf16[1024,384]{1,0:T(8,128)(2,1)} %collective-permute-done.1.x1, ...), custom_call_target="tpu_custom_call" | custom-call | flops 3221225472 | bytes 13631488 | tf_op jit(solution)/shard_map/pallas_call | solution.py:117
  (1 shorter events, 0.0 us)
Async XLA Ops:
  0.0 13.5 %collective-permute-start = (bf16[512,128]{1,0:T(8,128)(2,1)}, bf16[512,128]{1,0:T(8,128)(2,1)S(1)}, u32[]{:S(2)}, u32[]{:S(2)}) collective-permute-start(bf16[512,128]{1,0:T(8,128)(2,1)} %param.3), channel_id=1, source_target_pairs={{0,1},{1,0},{2,3},{3,2},{4,5},{5,4},{6,7},{7,6},{8,9},{9,8},{10,11... | collective-permute-start | bytes 393224 | tf_op jit(solution)/shard_map/ppermute | solution.py:28
  16.0 8.3 %copy-start = (bf16[256,1536]{1,0:T(8,128)(2,1)S(1)}, bf16[256,1536]{1,0:T(8,128)(2,1)}, u32[]{:S(2)}) copy-start(bf16[256,1536]{1,0:T(8,128)(2,1)} %param.4) | copy-start | bytes 2359300
  16.0 68.0 %all-to-all-start = ((bf16[8,512,256]{2,1,0:T(8,128)(2,1)}), bf16[8,512,256]{2,1,0:T(8,128)(2,1)S(1)}, u32[]{:S(2)}, u32[]{:S(2)}) async-start(bf16[8,512,256]{2,1,0:T(8,128)(2,1)} %broadcast_in_dim.2), calls=%async_computation | async-start | bytes 4194304 | tf_op jit(solution)/shard_map/all_to_all | solution.py:92
  43.6 33.4 %collective-permute-start.1 = (bf16[1024,384]{1,0:T(8,128)(2,1)S(1)}, bf16[1024,384]{1,0:T(8,128)(2,1)}, u32[]{:S(2)}, u32[]{:S(2)}) collective-permute-start(bf16[1024,384]{1,0:T(8,128)(2,1)S(1)} %all_gather.6.y0), channel_id=1, source_target_pairs={{0,128},{1,129},{2,130},{3,131},{4,132},{5,133},{6,134},{7,135},{8... | collective-permute-start | bytes 2359304 | tf_op jit(solution)/shard_map/ppermute | solution.py:28
  46.8 32.7 %collective-permute-start.2 = (bf16[1024,384]{1,0:T(8,128)(2,1)S(1)}, bf16[1024,384]{1,0:T(8,128)(2,1)}, u32[]{:S(2)}, u32[]{:S(2)}) collective-permute-start(bf16[1024,384]{1,0:T(8,128)(2,1)S(1)} %all_gather.6.y0), channel_id=1, source_target_pairs={{0,384},{1,385},{2,386},{3,387},{4,388},{5,389},{6,390},{7,391},{8... | collective-permute-start | bytes 2359304 | tf_op jit(solution)/shard_map/ppermute | solution.py:28
  66.8 14.7 %collective-permute-start.4 = (bf16[1024,384]{1,0:T(8,128)(2,1)}, bf16[1024,384]{1,0:T(8,128)(2,1)}, u32[]{:S(2)}, u32[]{:S(2)}) collective-permute-start(bf16[1024,384]{1,0:T(8,128)(2,1)} %all_gather.7.y2), channel_id=1, source_target_pairs={{0,16},{1,17},{2,18},{3,19},{4,20},{5,21},{6,22},{7,23},{8,24},{9,... | collective-permute-start | bytes 2359304 | tf_op jit(solution)/shard_map/ppermute | solution.py:28
  75.1 6.4 %collective-permute-start.3 = (bf16[1024,384]{1,0:T(8,128)(2,1)S(1)}, bf16[1024,384]{1,0:T(8,128)(2,1)}, u32[]{:S(2)}, u32[]{:S(2)}) collective-permute-start(bf16[1024,384]{1,0:T(8,128)(2,1)S(1)} %all_gather.6.y0), channel_id=1, source_target_pairs={{0,16},{1,17},{2,18},{3,19},{4,20},{5,21},{6,22},{7,23},{8,24},{9,... | collective-permute-start | bytes 2359304 | tf_op jit(solution)/shard_map/ppermute | solution.py:28
  77.1 4.6 %collective-permute-start.5 = (bf16[1024,384]{1,0:T(8,128)(2,1)}, bf16[1024,384]{1,0:T(8,128)(2,1)}, u32[]{:S(2)}, u32[]{:S(2)}) collective-permute-start(bf16[1024,384]{1,0:T(8,128)(2,1)} %collective-permute-done.1.x1), channel_id=1, source_target_pairs={{0,16},{1,17},{2,18},{3,19},{4,20},{5,21},{6,22},{7,23},{8,24},{9,... | collective-permute-start | bytes 2359304 | tf_op jit(solution)/shard_map/ppermute | solution.py:28
  79.5 4.5 %collective-permute-start.6 = (bf16[1024,384]{1,0:T(8,128)(2,1)}, bf16[1024,384]{1,0:T(8,128)(2,1)}, u32[]{:S(2)}, u32[]{:S(2)}) collective-permute-start(bf16[1024,384]{1,0:T(8,128)(2,1)} %collective-permute-done.2.x3), channel_id=1, source_target_pairs={{0,16},{1,17},{2,18},{3,19},{4,20},{5,21},{6,22},{7,23},{8,24},{9,... | collective-permute-start | bytes 2359304 | tf_op jit(solution)/shard_map/ppermute | solution.py:28

commit v4 on v3

--- a/solution.py
+++ b/solution.py
@@ -37,7 +37,7 @@
 
 
 def kernel(place, tokens, y0, y2, x1, x3, s0, s2, s1, s3, acc, out, w, sums, result, w_sem, a_sem, o_sem):
-    d, c = place[0], place[1]
+    d, c, yh = place[0], place[1], place[2]
     deep = YL * KB
 
     def start(source, target, sem):
@@ -69,13 +69,15 @@
             for side in range(2):
                 for k in range(YL):
                     block = w[p, side * deep + k * KB:side * deep + (k + 1) * KB]
-                    total += jnp.dot(
-                        tokens[k * CORES + lax.bitwise_xor(side, c), rows], block, preferred_element_type=jnp.float32)
+                    z = k * CORES + lax.bitwise_xor(side, c)
+                    features = jnp.concatenate([tokens[z, yh, rows], tokens[z, 1 - yh, rows]], axis=1)
+                    total += jnp.dot(features, block, preferred_element_type=jnp.float32)
             result[p, rows] = gelu(total).astype(jnp.bfloat16)
-        for i in range(2):
-            at = pl.multiple_of(lax.bitwise_xor(d, p + 2 * i) * Q, 128)
-            o_copies.append(start(
-                result.at[p, :, pl.ds(i * Q, Q)], out.at[:, pl.ds(at, Q)], o_sem.at[p * 2 + i]))
+            for i in range(2):
+                at = pl.multiple_of(lax.bitwise_xor(d, p + 2 * i) * Q, 128)
+                o_copies.append(start(
+                    result.at[p, pl.ds(m, 256), pl.ds(i * Q, Q)], out.at[pl.ds(m, 256), pl.ds(at, Q)],
+                    o_sem.at[p * 4 + m // 128 + i]))
     wait(o_copies)
 
 
@@ -87,9 +89,15 @@
     return lax.all_to_all(parts, "row", 0, 0, axis_index_groups=groups).reshape(YL * block.shape[0], block.shape[1])
 
 
-def along_z(parts):
+def fan(first, second):
+    parts = lax.optimization_barrier(jnp.broadcast_to(first[None, None], (Z, 2, *first.shape)))
+    block = jnp.broadcast_to(second[None, None], (Z, 1, *second.shape))
+    return lax.dynamic_update_slice(parts, block, (0, 1, 0, 0))
+
+
+def along_z(first, second):
     groups = [[z * YH + yh for z in range(Z)] for yh in range(YH)]
-    return lax.all_to_all(parts, "col", 0, 0, axis_index_groups=groups)
+    return lax.all_to_all(fan(first, second), "col", 0, 0, axis_index_groups=groups)
 
 
 def after(value, *others):
@@ -99,15 +107,13 @@
 def shards(t, w, acc):
     d, r, col = lax.axis_index("dp"), lax.axis_index("row"), lax.axis_index("col")
     yh = col % YH
-    place = jnp.stack([d, r % CORES]).astype(jnp.int32)
+    place = jnp.stack([d, r % CORES, yh]).astype(jnp.int32)
 
     def quarter(j):
         return lax.dynamic_slice(w, (0, lax.bitwise_xor(d, j) * Q), (KB, Q))
 
     t1 = send(t, lambda x, yl, c, z, yh: (x, yl, c, z, 1 - yh))
-    t0 = jnp.where(yh == 0, jnp.concatenate([t, t1], axis=1), jnp.concatenate([t1, t], axis=1))
-    parts = jnp.broadcast_to(t0[None], (Z, *t0.shape))
-    tokens = along_z(parts)
+    tokens = along_z(t, t1)
     y0 = along_y(quarter(0), True)
     x1 = send(y0, lambda x, yl, c, z, yh: (x ^ 1, yl, c, z, yh))
     x3 = send(y0, lambda x, yl, c, z, yh: (x ^ 3, yl, c, z, yh))
@@ -126,7 +132,7 @@
             pltpu.VMEM((2, TOK, 2 * Q), jnp.bfloat16),
             pltpu.SemaphoreType.DMA((8,)),
             pltpu.SemaphoreType.DMA((4,)),
-            pltpu.SemaphoreType.DMA((4,)),
+            pltpu.SemaphoreType.DMA((8,)),
         ],
         compiler_params=pltpu.CompilerParams(vmem_limit_bytes=44 * 1024 * 1024),
         cost_estimate=pl.CostEstimate(

time: 92.6 us -> 91.3 us (0.986)
  waiting for transfers between devices: 7.68 us -> 5.03 us
  local copies, waits for them, and re-layouts: 1.52 us -> 3.85 us
  other arithmetic: 1.13 us -> 0.08 us
    ppermute x7, waiting for transfers between devices: 7.68 us -> 5.03 us  [send(): return lax.ppermute(array, AXES, pairs)]
    broadcast_in_dim x1, local copies, waits for them, and re-layouts: 1.47 us -> 2.65 us  [fan(): jnp.broadcast_to(first[None, None], (Z, 2, *first.shape))]
    dynamic_update_slice x0 -> x1, local copies, waits for them, and re-layouts: none -> 1.14 us  [fan(): return lax.dynamic_update_slice(parts, block, (0, 1, 0, 0))]
    select_n x1 -> x0, other arithmetic: 1.05 us -> none  [shards(): jnp.where(yh == 0, jnp.concatenate([t, t1], axis=1), jnp.concatenate([t1,...]
  transfers between devices with their start and end apart: 8 -> 8, of which waited for: 3 -> 3; matrix products, arithmetic and copies ran while one was open for 0% -> 3% of each run, Pallas kernels for 0% -> 0%
where the time goes in v4:
time: 91.3 us; the launch traced here: 90.9 us
  starting transfers between devices  38 us (42%)
  blocking collectives  35.6 us (39%)
  Pallas kernels  8.27 us (9%)
  waiting for transfers between devices  5.03 us (6%)
  local copies, waits for them, and re-layouts  3.85 us (4%)
    all_gather x2, blocking collectives, along_y(): lax.all_gather(block, 'row', axis=0, tiled=True, axis_index_groups=groups)  35.6 us
    ppermute x7, starting transfers between devices, send(): return lax.ppermute(array, AXES, pairs)  29.7 us
    all_to_all x1, starting transfers between devices, along_z(): lax.all_to_all(fan(first, second), 'col', 0, 0, axis_index_groups=groups)  8.3 us
    pallas_call x1, Pallas kernels, shards(): pl.pallas_call(kernel, out_shape=jax.ShapeDtypeStruct((TOK, FF), jnp.bflo...  8.27 us
    ppermute x7, waiting for transfers between devices, send(): return lax.ppermute(array, AXES, pairs)  5.03 us
    broadcast_in_dim x1, local copies, waits for them, and re-layouts, fan(): jnp.broadcast_to(first[None, None], (Z, 2, *first.shape))  2.65 us
  transfers between devices with their start and end apart: 8, of which 3 were waited for; matrix products, arithmetic and copies ran while one was open for 3% of the time, Pallas kernels for 0%

profile of v4, /device:TPU:1, one launch (start us, length us, event | category | flops | bytes accessed | tf_op | source)
XLA Modules:
  0.0 90.9 jit_solution(5931265478712605283)
XLA Ops:
  0.0 8.3 %collective-permute-start = (bf16[512,128]{1,0:T(8,128)(2,1)}, bf16[512,128]{1,0:T(8,128)(2,1)S(1)}, u32[]{:S(2)}, u32[]{:S(2)}) collective-permute-start(bf16[512,128]{1,0:T(8,128)(2,1)} %param.3), channel_id=1, source_target_pairs={{0,1},{1,0},{2,3},{3,2},{4,5},{5,4},{6,7},{7,6},{8,9},{9,8},{10,11... | collective-permute-start | bytes 393224 | tf_op jit(solution)/shard_map/ppermute | solution.py:28
  8.3 2.7 %broadcast_in_dim.4 = bf16[8,2,512,128]{3,2,1,0:T(8,128)(2,1)} broadcast(bf16[512,128]{1,0:T(8,128)(2,1)} %param.3), dimensions={2,3} | broadcast | bytes 2228224 | tf_op jit(solution)/shard_map/broadcast_in_dim | solution.py:93
  10.9 2.5 %collective-permute-done = bf16[512,128]{1,0:T(8,128)(2,1)S(1)} collective-permute-done((bf16[512,128]{1,0:T(8,128)(2,1)}, bf16[512,128]{1,0:T(8,128)(2,1)S(1)}, u32[]{:S(2)}, u32[]{:S(2)}) %collective-permute-start) | collective-permute-done | bytes 131104 | tf_op jit(solution)/shard_map/ppermute | solution.py:28
  13.5 1.1 %broadcast_dynamic-update-slice_fusion = bf16[8,2,512,128]{3,2,1,0:T(8,128)(2,1)} fusion(bf16[8,2,512,128]{3,2,1,0:T(8,128)(2,1)} %broadcast_in_dim.4, bf16[512,128]{1,0:T(8,128)(2,1)S(1)} %collective-permute-done), kind=kLoop, calls=%fused_computation | loop fusion | bytes 1179648 | tf_op jit(solution)/shard_map/dynamic_update_slice | solution.py:95
  14.6 0.0 copy-start
  14.6 8.3 %all-to-all-start = ((bf16[8,2,512,128]{3,2,1,0:T(8,128)(2,1)}), bf16[8,2,512,128]{3,2,1,0:T(8,128)(2,1)S(1)}, u32[]{:S(2)}, u32[]{:S(2)}) async-start(bf16[8,2,512,128]{3,2,1,0:T(8,128)(2,1)} %broadcast_dynamic-update-slice_fusion), calls=%async_computation | async-start | bytes 4194304 | tf_op jit(solution)/shard_map/all_to_all | solution.py:100
  22.9 0.0 copy-done
  23.0 19.3 %all_gather.6.y0 = bf16[1024,384]{1,0:T(8,128)(2,1)S(1)} all-gather(bf16[256,384]{1,0:T(8,128)(2,1)S(1)} %get-tuple-element.10), channel_id=1, replica_groups={{0,32,64,96},{16,48,80,112},{1,33,65,97},{17,49,81,113},{2,34,66,98},{1..., dimensions={0}, use_global_device_ids=true | all-gather | bytes 983040 | tf_op jit(solution)/shard_map/all_gather | solution.py:87
  42.3 3.1 %collective-permute-start.1 = (bf16[1024,384]{1,0:T(8,128)(2,1)S(1)}, bf16[1024,384]{1,0:T(8,128)(2,1)}, u32[]{:S(2)}, u32[]{:S(2)}) collective-permute-start(bf16[1024,384]{1,0:T(8,128)(2,1)S(1)} %all_gather.6.y0), channel_id=1, source_target_pairs={{0,128},{1,129},{2,130},{3,131},{4,132},{5,133},{6,134},{7,135},{8... | collective-permute-start | bytes 2359304 | tf_op jit(solution)/shard_map/ppermute | solution.py:28
  45.4 3.7 %collective-permute-start.2 = (bf16[1024,384]{1,0:T(8,128)(2,1)S(1)}, bf16[1024,384]{1,0:T(8,128)(2,1)}, u32[]{:S(2)}, u32[]{:S(2)}) collective-permute-start(bf16[1024,384]{1,0:T(8,128)(2,1)S(1)} %all_gather.6.y0), channel_id=1, source_target_pairs={{0,384},{1,385},{2,386},{3,387},{4,388},{5,389},{6,390},{7,391},{8... | collective-permute-start | bytes 2359304 | tf_op jit(solution)/shard_map/ppermute | solution.py:28
  49.1 16.3 %all_gather.7.y2 = bf16[1024,384]{1,0:T(8,128)(2,1)} all-gather(bf16[256,384]{1,0:T(8,128)(2,1)S(1)} %get-tuple-element.7), channel_id=1, replica_groups={{0,32,64,96},{16,48,80,112},{1,33,65,97},{17,49,81,113},{2,34,66,98},{1..., dimensions={0}, use_global_device_ids=true | all-gather | bytes 983040 | tf_op jit(solution)/shard_map/all_gather | solution.py:87
  65.4 8.3 %collective-permute-start.4 = (bf16[1024,384]{1,0:T(8,128)(2,1)}, bf16[1024,384]{1,0:T(8,128)(2,1)}, u32[]{:S(2)}, u32[]{:S(2)}) collective-permute-start(bf16[1024,384]{1,0:T(8,128)(2,1)} %all_gather.7.y2), channel_id=1, source_target_pairs={{0,16},{1,17},{2,18},{3,19},{4,20},{5,21},{6,22},{7,23},{8,24},{9,... | collective-permute-start | bytes 2359304 | tf_op jit(solution)/shard_map/ppermute | solution.py:28
  73.7 1.9 %collective-permute-start.3 = (bf16[1024,384]{1,0:T(8,128)(2,1)S(1)}, bf16[1024,384]{1,0:T(8,128)(2,1)}, u32[]{:S(2)}, u32[]{:S(2)}) collective-permute-start(bf16[1024,384]{1,0:T(8,128)(2,1)S(1)} %all_gather.6.y0), channel_id=1, source_target_pairs={{0,16},{1,17},{2,18},{3,19},{4,20},{5,21},{6,22},{7,23},{8,24},{9,... | collective-permute-start | bytes 2359304 | tf_op jit(solution)/shard_map/ppermute | solution.py:28
  75.7 0.0 collective-permute-done.1.x1
  75.7 2.4 %collective-permute-start.5 = (bf16[1024,384]{1,0:T(8,128)(2,1)}, bf16[1024,384]{1,0:T(8,128)(2,1)}, u32[]{:S(2)}, u32[]{:S(2)}) collective-permute-start(bf16[1024,384]{1,0:T(8,128)(2,1)} %collective-permute-done.1.x1), channel_id=1, source_target_pairs={{0,16},{1,17},{2,18},{3,19},{4,20},{5,21},{6,22},{7,23},{8,24},{9,... | collective-permute-start | bytes 2359304 | tf_op jit(solution)/shard_map/ppermute | solution.py:28
  78.1 0.0 collective-permute-done.2.x3
  78.1 1.9 %collective-permute-start.6 = (bf16[1024,384]{1,0:T(8,128)(2,1)}, bf16[1024,384]{1,0:T(8,128)(2,1)}, u32[]{:S(2)}, u32[]{:S(2)}) collective-permute-start(bf16[1024,384]{1,0:T(8,128)(2,1)} %collective-permute-done.2.x3), channel_id=1, source_target_pairs={{0,16},{1,17},{2,18},{3,19},{4,20},{5,21},{6,22},{7,23},{8,24},{9,... | collective-permute-start | bytes 2359304 | tf_op jit(solution)/shard_map/ppermute | solution.py:28
  80.1 0.1 pad_add_fusion.place
  80.1 0.0 collective-permute-done.3.s0
  80.1 0.0 collective-permute-done.4.s2
  80.1 0.2 collective-permute-done.5.s1
  80.3 2.3 %collective-permute-done.6.s3 = bf16[1024,384]{1,0:T(8,128)(2,1)} collective-permute-done((bf16[1024,384]{1,0:T(8,128)(2,1)}, bf16[1024,384]{1,0:T(8,128)(2,1)}, u32[]{:S(2)}, u32[]{:S(2)}) %collective-permute-start.6) | collective-permute-done | bytes 786464 | tf_op jit(solution)/shard_map/ppermute | solution.py:28
  82.6 0.0 all-to-all-done.tokens
  82.6 8.3 %shard_map.37 = bf16[512,1536]{1,0:T(8,128)(2,1)} custom-call(s32[3]{0:T(128)S(1)} %pad_add_fusion.place, bf16[8,2,512,128]{3,2,1,0:T(8,128)(2,1)S(1)} %all-to-all-done.tokens, bf16[1024,384]{1,0:T(8,128)(2,1)S(1)} %all_gather.6.y0, bf16[1024,384]{1,0:T(8,128)(2,1)} %all_gather.7.y2, bf16[1024,384]{1,0:T(8,128)(2,1)} %collective-permute-done.1.x1, ...), custom_call_target="tpu_custom_call" | custom-call | flops 3221225472 | bytes 13631488 | tf_op jit(solution)/shard_map/pallas_call | solution.py:123
  (1 shorter events, 0.0 us)
Async XLA Ops:
  0.0 13.5 %collective-permute-start = (bf16[512,128]{1,0:T(8,128)(2,1)}, bf16[512,128]{1,0:T(8,128)(2,1)S(1)}, u32[]{:S(2)}, u32[]{:S(2)}) collective-permute-start(bf16[512,128]{1,0:T(8,128)(2,1)} %param.3), channel_id=1, source_target_pairs={{0,1},{1,0},{2,3},{3,2},{4,5},{5,4},{6,7},{7,6},{8,9},{9,8},{10,11... | collective-permute-start | bytes 393224 | tf_op jit(solution)/shard_map/ppermute | solution.py:28
  14.6 8.3 %copy-start = (bf16[256,1536]{1,0:T(8,128)(2,1)S(1)}, bf16[256,1536]{1,0:T(8,128)(2,1)}, u32[]{:S(2)}) copy-start(bf16[256,1536]{1,0:T(8,128)(2,1)} %param.4) | copy-start | bytes 2359300
  14.6 68.0 %all-to-all-start = ((bf16[8,2,512,128]{3,2,1,0:T(8,128)(2,1)}), bf16[8,2,512,128]{3,2,1,0:T(8,128)(2,1)S(1)}, u32[]{:S(2)}, u32[]{:S(2)}) async-start(bf16[8,2,512,128]{3,2,1,0:T(8,128)(2,1)} %broadcast_dynamic-update-slice_fusion), calls=%async_computation | async-start | bytes 4194304 | tf_op jit(solution)/shard_map/all_to_all | solution.py:100
  42.3 33.4 %collective-permute-start.1 = (bf16[1024,384]{1,0:T(8,128)(2,1)S(1)}, bf16[1024,384]{1,0:T(8,128)(2,1)}, u32[]{:S(2)}, u32[]{:S(2)}) collective-permute-start(bf16[1024,384]{1,0:T(8,128)(2,1)S(1)} %all_gather.6.y0), channel_id=1, source_target_pairs={{0,128},{1,129},{2,130},{3,131},{4,132},{5,133},{6,134},{7,135},{8... | collective-permute-start | bytes 2359304 | tf_op jit(solution)/shard_map/ppermute | solution.py:28
  45.4 32.7 %collective-permute-start.2 = (bf16[1024,384]{1,0:T(8,128)(2,1)S(1)}, bf16[1024,384]{1,0:T(8,128)(2,1)}, u32[]{:S(2)}, u32[]{:S(2)}) collective-permute-start(bf16[1024,384]{1,0:T(8,128)(2,1)S(1)} %all_gather.6.y0), channel_id=1, source_target_pairs={{0,384},{1,385},{2,386},{3,387},{4,388},{5,389},{6,390},{7,391},{8... | collective-permute-start | bytes 2359304 | tf_op jit(solution)/shard_map/ppermute | solution.py:28
  65.4 14.7 %collective-permute-start.4 = (bf16[1024,384]{1,0:T(8,128)(2,1)}, bf16[1024,384]{1,0:T(8,128)(2,1)}, u32[]{:S(2)}, u32[]{:S(2)}) collective-permute-start(bf16[1024,384]{1,0:T(8,128)(2,1)} %all_gather.7.y2), channel_id=1, source_target_pairs={{0,16},{1,17},{2,18},{3,19},{4,20},{5,21},{6,22},{7,23},{8,24},{9,... | collective-permute-start | bytes 2359304 | tf_op jit(solution)/shard_map/ppermute | solution.py:28
  73.7 6.4 %collective-permute-start.3 = (bf16[1024,384]{1,0:T(8,128)(2,1)S(1)}, bf16[1024,384]{1,0:T(8,128)(2,1)}, u32[]{:S(2)}, u32[]{:S(2)}) collective-permute-start(bf16[1024,384]{1,0:T(8,128)(2,1)S(1)} %all_gather.6.y0), channel_id=1, source_target_pairs={{0,16},{1,17},{2,18},{3,19},{4,20},{5,21},{6,22},{7,23},{8,24},{9,... | collective-permute-start | bytes 2359304 | tf_op jit(solution)/shard_map/ppermute | solution.py:28
  75.7 4.6 %collective-permute-start.5 = (bf16[1024,384]{1,0:T(8,128)(2,1)}, bf16[1024,384]{1,0:T(8,128)(2,1)}, u32[]{:S(2)}, u32[]{:S(2)}) collective-permute-start(bf16[1024,384]{1,0:T(8,128)(2,1)} %collective-permute-done.1.x1), channel_id=1, source_target_pairs={{0,16},{1,17},{2,18},{3,19},{4,20},{5,21},{6,22},{7,23},{8,24},{9,... | collective-permute-start | bytes 2359304 | tf_op jit(solution)/shard_map/ppermute | solution.py:28
  78.1 4.5 %collective-permute-start.6 = (bf16[1024,384]{1,0:T(8,128)(2,1)}, bf16[1024,384]{1,0:T(8,128)(2,1)}, u32[]{:S(2)}, u32[]{:S(2)}) collective-permute-start(bf16[1024,384]{1,0:T(8,128)(2,1)} %collective-permute-done.2.x3), channel_id=1, source_target_pairs={{0,16},{1,17},{2,18},{3,19},{4,20},{5,21},{6,22},{7,23},{8,24},{9,... | collective-permute-start | bytes 2359304 | tf_op jit(solution)/shard_map/ppermute | solution.py:28

commit v5 on v4

--- a/solution.py
+++ b/solution.py
@@ -52,32 +52,30 @@
     pairs = (((y0, s0), (y2, s2)), ((x1, s1), (x3, s3)))
     w_copies, a_copies = [], []
     for p in range(2):
-        w_copies.append([
-            start(pairs[p][i][side], w.at[p, pl.ds(side * deep, deep), pl.ds(i * Q, Q)], w_sem.at[p * 4 + side * 2 + i])
-            for side in range(2) for i in range(2)])
-        a_copies.append([
-            start(acc.at[:, pl.ds(pl.multiple_of(lax.bitwise_xor(d, p + 2 * i) * Q, 128), Q)],
-                  sums.at[p, :, pl.ds(i * Q, Q)], a_sem.at[p * 2 + i])
-            for i in range(2)])
+        for i in range(2):
+            w_copies.append([
+                start(pairs[p][i][side], w.at[p, pl.ds(side * deep, deep), pl.ds(i * Q, Q)], w_sem.at[p * 4 + side * 2 + i])
+                for side in range(2)])
+            at = pl.multiple_of(lax.bitwise_xor(d, p + 2 * i) * Q, 128)
+            a_copies.append([start(acc.at[:, pl.ds(at, Q)], sums.at[p, :, pl.ds(i * Q, Q)], a_sem.at[p * 2 + i])])
+    blocks = [k * CORES + lax.bitwise_xor(side, c) for side in range(2) for k in range(YL)]
     o_copies = []
-    for p in range(2):
-        wait(w_copies[p])
-        wait(a_copies[p])
+    for p, first, last, needs in ((0, 0, 256, (0,)), (0, 256, 2 * Q, (1,)), (1, 0, 2 * Q, (2, 3))):
+        for q in needs:
+            wait(w_copies[q])
+            wait(a_copies[q])
+        columns = slice(first, last)
         for m in range(0, TOK, 256):
             rows = slice(m, m + 256)
-            total = sums[p, rows]
-            for side in range(2):
-                for k in range(YL):
-                    block = w[p, side * deep + k * KB:side * deep + (k + 1) * KB]
-                    z = k * CORES + lax.bitwise_xor(side, c)
-                    features = jnp.concatenate([tokens[z, yh, rows], tokens[z, 1 - yh, rows]], axis=1)
-                    total += jnp.dot(features, block, preferred_element_type=jnp.float32)
-            result[p, rows] = gelu(total).astype(jnp.bfloat16)
-            for i in range(2):
-                at = pl.multiple_of(lax.bitwise_xor(d, p + 2 * i) * Q, 128)
-                o_copies.append(start(
-                    result.at[p, pl.ds(m, 256), pl.ds(i * Q, Q)], out.at[pl.ds(m, 256), pl.ds(at, Q)],
-                    o_sem.at[p * 4 + m // 128 + i]))
+            features = jnp.concatenate([tokens[z, half, rows] for z in blocks for half in (yh, 1 - yh)], axis=1)
+            total = sums[p, rows, columns] + jnp.dot(features, w[p, :, columns], preferred_element_type=jnp.float32)
+            result[p, rows, columns] = gelu(total).astype(jnp.bfloat16)
+            if last == 2 * Q:
+                for i in range(2):
+                    at = pl.multiple_of(lax.bitwise_xor(d, p + 2 * i) * Q, 128)
+                    o_copies.append(start(
+                        result.at[p, pl.ds(m, 256), pl.ds(i * Q, Q)], out.at[pl.ds(m, 256), pl.ds(at, Q)],
+                        o_sem.at[p * 4 + m // 128 + i]))
     wait(o_copies)
 
 

time: 91.3 us -> 90.7 us (level)
  no operation moved by 1% of the time
where the time goes in v5:
time: 90.7 us; the launch traced here: 90.3 us
  starting transfers between devices  38 us (42%)
  blocking collectives  35.6 us (39%)
  Pallas kernels  7.67 us (8%)
  waiting for transfers between devices  5.03 us (6%)
  local copies, waits for them, and re-layouts  3.85 us (4%)
    all_gather x2, blocking collectives, along_y(): lax.all_gather(block, 'row', axis=0, tiled=True, axis_index_groups=groups)  35.6 us
    ppermute x7, starting transfers between devices, send(): return lax.ppermute(array, AXES, pairs)  29.7 us
    all_to_all x1, starting transfers between devices, along_z(): lax.all_to_all(fan(first, second), 'col', 0, 0, axis_index_groups=groups)  8.3 us
    pallas_call x1, Pallas kernels, shards(): pl.pallas_call(kernel, out_shape=jax.ShapeDtypeStruct((TOK, FF), jnp.bflo...  7.67 us
    ppermute x7, waiting for transfers between devices, send(): return lax.ppermute(array, AXES, pairs)  5.03 us
    broadcast_in_dim x1, local copies, waits for them, and re-layouts, fan(): jnp.broadcast_to(first[None, None], (Z, 2, *first.shape))  2.65 us
  transfers between devices with their start and end apart: 8, of which 3 were waited for; matrix products, arithmetic and copies ran while one was open for 3% of the time, Pallas kernels for 0%

profile of v5, /device:TPU:1, one launch (start us, length us, event | category | flops | bytes accessed | tf_op | source)
XLA Modules:
  0.0 90.3 jit_solution(264181026584292316)
XLA Ops:
  0.0 8.3 %collective-permute-start = (bf16[512,128]{1,0:T(8,128)(2,1)}, bf16[512,128]{1,0:T(8,128)(2,1)S(1)}, u32[]{:S(2)}, u32[]{:S(2)}) collective-permute-start(bf16[512,128]{1,0:T(8,128)(2,1)} %param.3), channel_id=1, source_target_pairs={{0,1},{1,0},{2,3},{3,2},{4,5},{5,4},{6,7},{7,6},{8,9},{9,8},{10,11... | collective-permute-start | bytes 393224 | tf_op jit(solution)/shard_map/ppermute | solution.py:28
  8.3 2.7 %broadcast_in_dim.4 = bf16[8,2,512,128]{3,2,1,0:T(8,128)(2,1)} broadcast(bf16[512,128]{1,0:T(8,128)(2,1)} %param.3), dimensions={2,3} | broadcast | bytes 2228224 | tf_op jit(solution)/shard_map/broadcast_in_dim | solution.py:91
  10.9 2.5 %collective-permute-done = bf16[512,128]{1,0:T(8,128)(2,1)S(1)} collective-permute-done((bf16[512,128]{1,0:T(8,128)(2,1)}, bf16[512,128]{1,0:T(8,128)(2,1)S(1)}, u32[]{:S(2)}, u32[]{:S(2)}) %collective-permute-start) | collective-permute-done | bytes 131104 | tf_op jit(solution)/shard_map/ppermute | solution.py:28
  13.5 1.1 %broadcast_dynamic-update-slice_fusion = bf16[8,2,512,128]{3,2,1,0:T(8,128)(2,1)} fusion(bf16[8,2,512,128]{3,2,1,0:T(8,128)(2,1)} %broadcast_in_dim.4, bf16[512,128]{1,0:T(8,128)(2,1)S(1)} %collective-permute-done), kind=kLoop, calls=%fused_computation | loop fusion | bytes 1179648 | tf_op jit(solution)/shard_map/dynamic_update_slice | solution.py:93
  14.6 0.0 copy-start
  14.6 8.3 %all-to-all-start = ((bf16[8,2,512,128]{3,2,1,0:T(8,128)(2,1)}), bf16[8,2,512,128]{3,2,1,0:T(8,128)(2,1)S(1)}, u32[]{:S(2)}, u32[]{:S(2)}) async-start(bf16[8,2,512,128]{3,2,1,0:T(8,128)(2,1)} %broadcast_dynamic-update-slice_fusion), calls=%async_computation | async-start | bytes 4194304 | tf_op jit(solution)/shard_map/all_to_all | solution.py:98
  22.9 0.0 copy-done
  23.0 19.3 %all_gather.6.y0 = bf16[1024,384]{1,0:T(8,128)(2,1)S(1)} all-gather(bf16[256,384]{1,0:T(8,128)(2,1)S(1)} %get-tuple-element.10), channel_id=1, replica_groups={{0,32,64,96},{16,48,80,112},{1,33,65,97},{17,49,81,113},{2,34,66,98},{1..., dimensions={0}, use_global_device_ids=true | all-gather | bytes 983040 | tf_op jit(solution)/shard_map/all_gather | solution.py:85
  42.3 3.1 %collective-permute-start.1 = (bf16[1024,384]{1,0:T(8,128)(2,1)S(1)}, bf16[1024,384]{1,0:T(8,128)(2,1)}, u32[]{:S(2)}, u32[]{:S(2)}) collective-permute-start(bf16[1024,384]{1,0:T(8,128)(2,1)S(1)} %all_gather.6.y0), channel_id=1, source_target_pairs={{0,128},{1,129},{2,130},{3,131},{4,132},{5,133},{6,134},{7,135},{8... | collective-permute-start | bytes 2359304 | tf_op jit(solution)/shard_map/ppermute | solution.py:28
  45.4 3.7 %collective-permute-start.2 = (bf16[1024,384]{1,0:T(8,128)(2,1)S(1)}, bf16[1024,384]{1,0:T(8,128)(2,1)}, u32[]{:S(2)}, u32[]{:S(2)}) collective-permute-start(bf16[1024,384]{1,0:T(8,128)(2,1)S(1)} %all_gather.6.y0), channel_id=1, source_target_pairs={{0,384},{1,385},{2,386},{3,387},{4,388},{5,389},{6,390},{7,391},{8... | collective-permute-start | bytes 2359304 | tf_op jit(solution)/shard_map/ppermute | solution.py:28
  49.1 16.3 %all_gather.7.y2 = bf16[1024,384]{1,0:T(8,128)(2,1)} all-gather(bf16[256,384]{1,0:T(8,128)(2,1)S(1)} %get-tuple-element.7), channel_id=1, replica_groups={{0,32,64,96},{16,48,80,112},{1,33,65,97},{17,49,81,113},{2,34,66,98},{1..., dimensions={0}, use_global_device_ids=true | all-gather | bytes 983040 | tf_op jit(solution)/shard_map/all_gather | solution.py:85
  65.4 8.3 %collective-permute-start.4 = (bf16[1024,384]{1,0:T(8,128)(2,1)}, bf16[1024,384]{1,0:T(8,128)(2,1)}, u32[]{:S(2)}, u32[]{:S(2)}) collective-permute-start(bf16[1024,384]{1,0:T(8,128)(2,1)} %all_gather.7.y2), channel_id=1, source_target_pairs={{0,16},{1,17},{2,18},{3,19},{4,20},{5,21},{6,22},{7,23},{8,24},{9,... | collective-permute-start | bytes 2359304 | tf_op jit(solution)/shard_map/ppermute | solution.py:28
  73.7 1.9 %collective-permute-start.3 = (bf16[1024,384]{1,0:T(8,128)(2,1)S(1)}, bf16[1024,384]{1,0:T(8,128)(2,1)}, u32[]{:S(2)}, u32[]{:S(2)}) collective-permute-start(bf16[1024,384]{1,0:T(8,128)(2,1)S(1)} %all_gather.6.y0), channel_id=1, source_target_pairs={{0,16},{1,17},{2,18},{3,19},{4,20},{5,21},{6,22},{7,23},{8,24},{9,... | collective-permute-start | bytes 2359304 | tf_op jit(solution)/shard_map/ppermute | solution.py:28
  75.7 0.0 collective-permute-done.1.x1
  75.7 2.4 %collective-permute-start.5 = (bf16[1024,384]{1,0:T(8,128)(2,1)}, bf16[1024,384]{1,0:T(8,128)(2,1)}, u32[]{:S(2)}, u32[]{:S(2)}) collective-permute-start(bf16[1024,384]{1,0:T(8,128)(2,1)} %collective-permute-done.1.x1), channel_id=1, source_target_pairs={{0,16},{1,17},{2,18},{3,19},{4,20},{5,21},{6,22},{7,23},{8,24},{9,... | collective-permute-start | bytes 2359304 | tf_op jit(solution)/shard_map/ppermute | solution.py:28
  78.1 0.0 collective-permute-done.2.x3
  78.1 1.9 %collective-permute-start.6 = (bf16[1024,384]{1,0:T(8,128)(2,1)}, bf16[1024,384]{1,0:T(8,128)(2,1)}, u32[]{:S(2)}, u32[]{:S(2)}) collective-permute-start(bf16[1024,384]{1,0:T(8,128)(2,1)} %collective-permute-done.2.x3), channel_id=1, source_target_pairs={{0,16},{1,17},{2,18},{3,19},{4,20},{5,21},{6,22},{7,23},{8,24},{9,... | collective-permute-start | bytes 2359304 | tf_op jit(solution)/shard_map/ppermute | solution.py:28
  80.1 0.1 pad_add_fusion.place
  80.1 0.0 collective-permute-done.3.s0
  80.1 0.0 collective-permute-done.4.s2
  80.1 0.2 collective-permute-done.5.s1
  80.3 2.3 %collective-permute-done.6.s3 = bf16[1024,384]{1,0:T(8,128)(2,1)} collective-permute-done((bf16[1024,384]{1,0:T(8,128)(2,1)}, bf16[1024,384]{1,0:T(8,128)(2,1)}, u32[]{:S(2)}, u32[]{:S(2)}) %collective-permute-start.6) | collective-permute-done | bytes 786464 | tf_op jit(solution)/shard_map/ppermute | solution.py:28
  82.6 0.0 all-to-all-done.tokens
  82.6 7.7 %shard_map.37 = bf16[512,1536]{1,0:T(8,128)(2,1)} custom-call(s32[3]{0:T(128)S(1)} %pad_add_fusion.place, bf16[8,2,512,128]{3,2,1,0:T(8,128)(2,1)S(1)} %all-to-all-done.tokens, bf16[1024,384]{1,0:T(8,128)(2,1)S(1)} %all_gather.6.y0, bf16[1024,384]{1,0:T(8,128)(2,1)} %all_gather.7.y2, bf16[1024,384]{1,0:T(8,128)(2,1)} %collective-permute-done.1.x1, ...), custom_call_target="tpu_custom_call" | custom-call | flops 3221225472 | bytes 13631488 | tf_op jit(solution)/shard_map/pallas_call | solution.py:121
  (1 shorter events, 0.0 us)
Async XLA Ops:
  0.0 13.5 %collective-permute-start = (bf16[512,128]{1,0:T(8,128)(2,1)}, bf16[512,128]{1,0:T(8,128)(2,1)S(1)}, u32[]{:S(2)}, u32[]{:S(2)}) collective-permute-start(bf16[512,128]{1,0:T(8,128)(2,1)} %param.3), channel_id=1, source_target_pairs={{0,1},{1,0},{2,3},{3,2},{4,5},{5,4},{6,7},{7,6},{8,9},{9,8},{10,11... | collective-permute-start | bytes 393224 | tf_op jit(solution)/shard_map/ppermute | solution.py:28
  14.6 8.3 %copy-start = (bf16[256,1536]{1,0:T(8,128)(2,1)S(1)}, bf16[256,1536]{1,0:T(8,128)(2,1)}, u32[]{:S(2)}) copy-start(bf16[256,1536]{1,0:T(8,128)(2,1)} %param.4) | copy-start | bytes 2359300
  14.6 68.0 %all-to-all-start = ((bf16[8,2,512,128]{3,2,1,0:T(8,128)(2,1)}), bf16[8,2,512,128]{3,2,1,0:T(8,128)(2,1)S(1)}, u32[]{:S(2)}, u32[]{:S(2)}) async-start(bf16[8,2,512,128]{3,2,1,0:T(8,128)(2,1)} %broadcast_dynamic-update-slice_fusion), calls=%async_computation | async-start | bytes 4194304 | tf_op jit(solution)/shard_map/all_to_all | solution.py:98
  42.3 33.4 %collective-permute-start.1 = (bf16[1024,384]{1,0:T(8,128)(2,1)S(1)}, bf16[1024,384]{1,0:T(8,128)(2,1)}, u32[]{:S(2)}, u32[]{:S(2)}) collective-permute-start(bf16[1024,384]{1,0:T(8,128)(2,1)S(1)} %all_gather.6.y0), channel_id=1, source_target_pairs={{0,128},{1,129},{2,130},{3,131},{4,132},{5,133},{6,134},{7,135},{8... | collective-permute-start | bytes 2359304 | tf_op jit(solution)/shard_map/ppermute | solution.py:28
  45.4 32.7 %collective-permute-start.2 = (bf16[1024,384]{1,0:T(8,128)(2,1)S(1)}, bf16[1024,384]{1,0:T(8,128)(2,1)}, u32[]{:S(2)}, u32[]{:S(2)}) collective-permute-start(bf16[1024,384]{1,0:T(8,128)(2,1)S(1)} %all_gather.6.y0), channel_id=1, source_target_pairs={{0,384},{1,385},{2,386},{3,387},{4,388},{5,389},{6,390},{7,391},{8... | collective-permute-start | bytes 2359304 | tf_op jit(solution)/shard_map/ppermute | solution.py:28
  65.4 14.7 %collective-permute-start.4 = (bf16[1024,384]{1,0:T(8,128)(2,1)}, bf16[1024,384]{1,0:T(8,128)(2,1)}, u32[]{:S(2)}, u32[]{:S(2)}) collective-permute-start(bf16[1024,384]{1,0:T(8,128)(2,1)} %all_gather.7.y2), channel_id=1, source_target_pairs={{0,16},{1,17},{2,18},{3,19},{4,20},{5,21},{6,22},{7,23},{8,24},{9,... | collective-permute-start | bytes 2359304 | tf_op jit(solution)/shard_map/ppermute | solution.py:28
  73.7 6.4 %collective-permute-start.3 = (bf16[1024,384]{1,0:T(8,128)(2,1)S(1)}, bf16[1024,384]{1,0:T(8,128)(2,1)}, u32[]{:S(2)}, u32[]{:S(2)}) collective-permute-start(bf16[1024,384]{1,0:T(8,128)(2,1)S(1)} %all_gather.6.y0), channel_id=1, source_target_pairs={{0,16},{1,17},{2,18},{3,19},{4,20},{5,21},{6,22},{7,23},{8,24},{9,... | collective-permute-start | bytes 2359304 | tf_op jit(solution)/shard_map/ppermute | solution.py:28
  75.7 4.6 %collective-permute-start.5 = (bf16[1024,384]{1,0:T(8,128)(2,1)}, bf16[1024,384]{1,0:T(8,128)(2,1)}, u32[]{:S(2)}, u32[]{:S(2)}) collective-permute-start(bf16[1024,384]{1,0:T(8,128)(2,1)} %collective-permute-done.1.x1), channel_id=1, source_target_pairs={{0,16},{1,17},{2,18},{3,19},{4,20},{5,21},{6,22},{7,23},{8,24},{9,... | collective-permute-start | bytes 2359304 | tf_op jit(solution)/shard_map/ppermute | solution.py:28
  78.1 4.5 %collective-permute-start.6 = (bf16[1024,384]{1,0:T(8,128)(2,1)}, bf16[1024,384]{1,0:T(8,128)(2,1)}, u32[]{:S(2)}, u32[]{:S(2)}) collective-permute-start(bf16[1024,384]{1,0:T(8,128)(2,1)} %collective-permute-done.2.x3), channel_id=1, source_target_pairs={{0,16},{1,17},{2,18},{3,19},{4,20},{5,21},{6,22},{7,23},{8,24},{9,... | collective-permute-start | bytes 2359304 | tf_op jit(solution)/shard_map/ppermute | solution.py:28

commit v6 on v5

--- a/solution.py
+++ b/solution.py
@@ -56,7 +56,7 @@
             w_copies.append([
                 start(pairs[p][i][side], w.at[p, pl.ds(side * deep, deep), pl.ds(i * Q, Q)], w_sem.at[p * 4 + side * 2 + i])
                 for side in range(2)])
-            at = pl.multiple_of(lax.bitwise_xor(d, p + 2 * i) * Q, 128)
+            at = pl.multiple_of(lax.rem(d + p + 2 * i, X) * Q, 128)
             a_copies.append([start(acc.at[:, pl.ds(at, Q)], sums.at[p, :, pl.ds(i * Q, Q)], a_sem.at[p * 2 + i])])
     blocks = [k * CORES + lax.bitwise_xor(side, c) for side in range(2) for k in range(YL)]
     o_copies = []
@@ -72,7 +72,7 @@
             result[p, rows, columns] = gelu(total).astype(jnp.bfloat16)
             if last == 2 * Q:
                 for i in range(2):
-                    at = pl.multiple_of(lax.bitwise_xor(d, p + 2 * i) * Q, 128)
+                    at = pl.multiple_of(lax.rem(d + p + 2 * i, X) * Q, 128)
                     o_copies.append(start(
                         result.at[p, pl.ds(m, 256), pl.ds(i * Q, Q)], out.at[pl.ds(m, 256), pl.ds(at, Q)],
                         o_sem.at[p * 4 + m // 128 + i]))
@@ -108,13 +108,13 @@
     place = jnp.stack([d, r % CORES, yh]).astype(jnp.int32)
 
     def quarter(j):
-        return lax.dynamic_slice(w, (0, lax.bitwise_xor(d, j) * Q), (KB, Q))
+        return lax.dynamic_slice(w, (0, lax.rem(d + j, X) * Q), (KB, Q))
 
     t1 = send(t, lambda x, yl, c, z, yh: (x, yl, c, z, 1 - yh))
     tokens = along_z(t, t1)
     y0 = along_y(quarter(0), True)
-    x1 = send(y0, lambda x, yl, c, z, yh: (x ^ 1, yl, c, z, yh))
-    x3 = send(y0, lambda x, yl, c, z, yh: (x ^ 3, yl, c, z, yh))
+    x1 = send(y0, lambda x, yl, c, z, yh: (x - 1, yl, c, z, yh))
+    x3 = send(y0, lambda x, yl, c, z, yh: (x + 1, yl, c, z, yh))
     y2 = along_y(after(quarter(2), y0), True)
     s0, s2, s1, s3 = (swap(a) for a in (after(y0, y2), y2, x1, x3))
 

time: 90.7 us -> 89.8 us (0.990)
  starting transfers between devices: 38 us -> 36.8 us
    ppermute x7, starting transfers between devices: 29.7 us -> 28.5 us  [send(): return lax.ppermute(array, AXES, pairs)]
where the time goes in v6:
time: 89.8 us; the launch traced here: 89.4 us
  starting transfers between devices  36.8 us (41%)
  blocking collectives  35.9 us (40%)
  Pallas kernels  7.67 us (9%)
  waiting for transfers between devices  5.03 us (6%)
  local copies, waits for them, and re-layouts  3.85 us (4%)
    all_gather x2, blocking collectives, along_y(): lax.all_gather(block, 'row', axis=0, tiled=True, axis_index_groups=groups)  35.9 us
    ppermute x7, starting transfers between devices, send(): return lax.ppermute(array, AXES, pairs)  28.5 us
    all_to_all x1, starting transfers between devices, along_z(): lax.all_to_all(fan(first, second), 'col', 0, 0, axis_index_groups=groups)  8.3 us
    pallas_call x1, Pallas kernels, shards(): pl.pallas_call(kernel, out_shape=jax.ShapeDtypeStruct((TOK, FF), jnp.bflo...  7.67 us
    ppermute x7, waiting for transfers between devices, send(): return lax.ppermute(array, AXES, pairs)  5.03 us
    broadcast_in_dim x1, local copies, waits for them, and re-layouts, fan(): jnp.broadcast_to(first[None, None], (Z, 2, *first.shape))  2.65 us
  transfers between devices with their start and end apart: 8, of which 3 were waited for; matrix products, arithmetic and copies ran while one was open for 3% of the time, Pallas kernels for 0%

profile of v6, /device:TPU:1, one launch (start us, length us, event | category | flops | bytes accessed | tf_op | source)
XLA Modules:
  0.0 89.4 jit_solution(11999637793661412969)
XLA Ops:
  0.0 8.3 %collective-permute-start = (bf16[512,128]{1,0:T(8,128)(2,1)}, bf16[512,128]{1,0:T(8,128)(2,1)S(1)}, u32[]{:S(2)}, u32[]{:S(2)}) collective-permute-start(bf16[512,128]{1,0:T(8,128)(2,1)} %param.3), channel_id=1, source_target_pairs={{0,1},{1,0},{2,3},{3,2},{4,5},{5,4},{6,7},{7,6},{8,9},{9,8},{10,11... | collective-permute-start | bytes 393224 | tf_op jit(solution)/shard_map/ppermute | solution.py:28
  8.3 2.7 %broadcast_in_dim.4 = bf16[8,2,512,128]{3,2,1,0:T(8,128)(2,1)} broadcast(bf16[512,128]{1,0:T(8,128)(2,1)} %param.3), dimensions={2,3} | broadcast | bytes 2228224 | tf_op jit(solution)/shard_map/broadcast_in_dim | solution.py:91
  10.9 2.5 %collective-permute-done = bf16[512,128]{1,0:T(8,128)(2,1)S(1)} collective-permute-done((bf16[512,128]{1,0:T(8,128)(2,1)}, bf16[512,128]{1,0:T(8,128)(2,1)S(1)}, u32[]{:S(2)}, u32[]{:S(2)}) %collective-permute-start) | collective-permute-done | bytes 131104 | tf_op jit(solution)/shard_map/ppermute | solution.py:28
  13.5 1.1 %broadcast_dynamic-update-slice_fusion = bf16[8,2,512,128]{3,2,1,0:T(8,128)(2,1)} fusion(bf16[8,2,512,128]{3,2,1,0:T(8,128)(2,1)} %broadcast_in_dim.4, bf16[512,128]{1,0:T(8,128)(2,1)S(1)} %collective-permute-done), kind=kLoop, calls=%fused_computation | loop fusion | bytes 1179648 | tf_op jit(solution)/shard_map/dynamic_update_slice | solution.py:93
  14.6 0.0 copy-start
  14.6 8.3 %all-to-all-start = ((bf16[8,2,512,128]{3,2,1,0:T(8,128)(2,1)}), bf16[8,2,512,128]{3,2,1,0:T(8,128)(2,1)S(1)}, u32[]{:S(2)}, u32[]{:S(2)}) async-start(bf16[8,2,512,128]{3,2,1,0:T(8,128)(2,1)} %broadcast_dynamic-update-slice_fusion), calls=%async_computation | async-start | bytes 4194304 | tf_op jit(solution)/shard_map/all_to_all | solution.py:98
  22.9 0.0 copy-done
  23.0 19.3 %all_gather.6.y0 = bf16[1024,384]{1,0:T(8,128)(2,1)S(1)} all-gather(bf16[256,384]{1,0:T(8,128)(2,1)S(1)} %get-tuple-element.10), channel_id=1, replica_groups={{0,32,64,96},{16,48,80,112},{1,33,65,97},{17,49,81,113},{2,34,66,98},{1..., dimensions={0}, use_global_device_ids=true | all-gather | bytes 983040 | tf_op jit(solution)/shard_map/all_gather | solution.py:85
  42.3 4.4 %collective-permute-start.1 = (bf16[1024,384]{1,0:T(8,128)(2,1)S(1)}, bf16[1024,384]{1,0:T(8,128)(2,1)}, u32[]{:S(2)}, u32[]{:S(2)}) collective-permute-start(bf16[1024,384]{1,0:T(8,128)(2,1)S(1)} %all_gather.6.y0), channel_id=1, source_target_pairs={{0,384},{1,385},{2,386},{3,387},{4,388},{5,389},{6,390},{7,391},{8... | collective-permute-start | bytes 2359304 | tf_op jit(solution)/shard_map/ppermute | solution.py:28
  46.6 1.9 %collective-permute-start.2 = (bf16[1024,384]{1,0:T(8,128)(2,1)S(1)}, bf16[1024,384]{1,0:T(8,128)(2,1)}, u32[]{:S(2)}, u32[]{:S(2)}) collective-permute-start(bf16[1024,384]{1,0:T(8,128)(2,1)S(1)} %all_gather.6.y0), channel_id=1, source_target_pairs={{0,128},{1,129},{2,130},{3,131},{4,132},{5,133},{6,134},{7,135},{8... | collective-permute-start | bytes 2359304 | tf_op jit(solution)/shard_map/ppermute | solution.py:28
  48.6 16.6 %all_gather.7.y2 = bf16[1024,384]{1,0:T(8,128)(2,1)} all-gather(bf16[256,384]{1,0:T(8,128)(2,1)S(1)} %get-tuple-element.7), channel_id=1, replica_groups={{0,32,64,96},{16,48,80,112},{1,33,65,97},{17,49,81,113},{2,34,66,98},{1..., dimensions={0}, use_global_device_ids=true | all-gather | bytes 983040 | tf_op jit(solution)/shard_map/all_gather | solution.py:85
  65.2 7.7 %collective-permute-start.4 = (bf16[1024,384]{1,0:T(8,128)(2,1)}, bf16[1024,384]{1,0:T(8,128)(2,1)}, u32[]{:S(2)}, u32[]{:S(2)}) collective-permute-start(bf16[1024,384]{1,0:T(8,128)(2,1)} %all_gather.7.y2), channel_id=1, source_target_pairs={{0,16},{1,17},{2,18},{3,19},{4,20},{5,21},{6,22},{7,23},{8,24},{9,... | collective-permute-start | bytes 2359304 | tf_op jit(solution)/shard_map/ppermute | solution.py:28
  72.8 1.9 %collective-permute-start.3 = (bf16[1024,384]{1,0:T(8,128)(2,1)S(1)}, bf16[1024,384]{1,0:T(8,128)(2,1)}, u32[]{:S(2)}, u32[]{:S(2)}) collective-permute-start(bf16[1024,384]{1,0:T(8,128)(2,1)S(1)} %all_gather.6.y0), channel_id=1, source_target_pairs={{0,16},{1,17},{2,18},{3,19},{4,20},{5,21},{6,22},{7,23},{8,24},{9,... | collective-permute-start | bytes 2359304 | tf_op jit(solution)/shard_map/ppermute | solution.py:28
  74.8 0.0 collective-permute-done.1.x1
  74.8 2.4 %collective-permute-start.5 = (bf16[1024,384]{1,0:T(8,128)(2,1)}, bf16[1024,384]{1,0:T(8,128)(2,1)}, u32[]{:S(2)}, u32[]{:S(2)}) collective-permute-start(bf16[1024,384]{1,0:T(8,128)(2,1)} %collective-permute-done.1.x1), channel_id=1, source_target_pairs={{0,16},{1,17},{2,18},{3,19},{4,20},{5,21},{6,22},{7,23},{8,24},{9,... | collective-permute-start | bytes 2359304 | tf_op jit(solution)/shard_map/ppermute | solution.py:28
  77.2 0.0 collective-permute-done.2.x3
  77.2 1.9 %collective-permute-start.6 = (bf16[1024,384]{1,0:T(8,128)(2,1)}, bf16[1024,384]{1,0:T(8,128)(2,1)}, u32[]{:S(2)}, u32[]{:S(2)}) collective-permute-start(bf16[1024,384]{1,0:T(8,128)(2,1)} %collective-permute-done.2.x3), channel_id=1, source_target_pairs={{0,16},{1,17},{2,18},{3,19},{4,20},{5,21},{6,22},{7,23},{8,24},{9,... | collective-permute-start | bytes 2359304 | tf_op jit(solution)/shard_map/ppermute | solution.py:28
  79.1 0.1 pad_add_fusion.place
  79.2 0.0 collective-permute-done.3.s0
  79.2 0.0 collective-permute-done.4.s2
  79.2 0.2 collective-permute-done.5.s1
  79.4 2.3 %collective-permute-done.6.s3 = bf16[1024,384]{1,0:T(8,128)(2,1)} collective-permute-done((bf16[1024,384]{1,0:T(8,128)(2,1)}, bf16[1024,384]{1,0:T(8,128)(2,1)}, u32[]{:S(2)}, u32[]{:S(2)}) %collective-permute-start.6) | collective-permute-done | bytes 786464 | tf_op jit(solution)/shard_map/ppermute | solution.py:28
  81.7 0.0 all-to-all-done.tokens
  81.7 7.7 %shard_map.37 = bf16[512,1536]{1,0:T(8,128)(2,1)} custom-call(s32[3]{0:T(128)S(1)} %pad_add_fusion.place, bf16[8,2,512,128]{3,2,1,0:T(8,128)(2,1)S(1)} %all-to-all-done.tokens, bf16[1024,384]{1,0:T(8,128)(2,1)S(1)} %all_gather.6.y0, bf16[1024,384]{1,0:T(8,128)(2,1)} %all_gather.7.y2, bf16[1024,384]{1,0:T(8,128)(2,1)} %collective-permute-done.1.x1, ...), custom_call_target="tpu_custom_call" | custom-call | flops 3221225472 | bytes 13631488 | tf_op jit(solution)/shard_map/pallas_call | solution.py:121
  (1 shorter events, 0.0 us)
Async XLA Ops:
  0.0 13.5 %collective-permute-start = (bf16[512,128]{1,0:T(8,128)(2,1)}, bf16[512,128]{1,0:T(8,128)(2,1)S(1)}, u32[]{:S(2)}, u32[]{:S(2)}) collective-permute-start(bf16[512,128]{1,0:T(8,128)(2,1)} %param.3), channel_id=1, source_target_pairs={{0,1},{1,0},{2,3},{3,2},{4,5},{5,4},{6,7},{7,6},{8,9},{9,8},{10,11... | collective-permute-start | bytes 393224 | tf_op jit(solution)/shard_map/ppermute | solution.py:28
  14.6 8.3 %copy-start = (bf16[256,1536]{1,0:T(8,128)(2,1)S(1)}, bf16[256,1536]{1,0:T(8,128)(2,1)}, u32[]{:S(2)}) copy-start(bf16[256,1536]{1,0:T(8,128)(2,1)} %param.4) | copy-start | bytes 2359300
  14.6 67.1 %all-to-all-start = ((bf16[8,2,512,128]{3,2,1,0:T(8,128)(2,1)}), bf16[8,2,512,128]{3,2,1,0:T(8,128)(2,1)S(1)}, u32[]{:S(2)}, u32[]{:S(2)}) async-start(bf16[8,2,512,128]{3,2,1,0:T(8,128)(2,1)} %broadcast_dynamic-update-slice_fusion), calls=%async_computation | async-start | bytes 4194304 | tf_op jit(solution)/shard_map/all_to_all | solution.py:98
  42.3 32.5 %collective-permute-start.1 = (bf16[1024,384]{1,0:T(8,128)(2,1)S(1)}, bf16[1024,384]{1,0:T(8,128)(2,1)}, u32[]{:S(2)}, u32[]{:S(2)}) collective-permute-start(bf16[1024,384]{1,0:T(8,128)(2,1)S(1)} %all_gather.6.y0), channel_id=1, source_target_pairs={{0,384},{1,385},{2,386},{3,387},{4,388},{5,389},{6,390},{7,391},{8... | collective-permute-start | bytes 2359304 | tf_op jit(solution)/shard_map/ppermute | solution.py:28
  46.6 30.6 %collective-permute-start.2 = (bf16[1024,384]{1,0:T(8,128)(2,1)S(1)}, bf16[1024,384]{1,0:T(8,128)(2,1)}, u32[]{:S(2)}, u32[]{:S(2)}) collective-permute-start(bf16[1024,384]{1,0:T(8,128)(2,1)S(1)} %all_gather.6.y0), channel_id=1, source_target_pairs={{0,128},{1,129},{2,130},{3,131},{4,132},{5,133},{6,134},{7,135},{8... | collective-permute-start | bytes 2359304 | tf_op jit(solution)/shard_map/ppermute | solution.py:28
  65.2 14.1 %collective-permute-start.4 = (bf16[1024,384]{1,0:T(8,128)(2,1)}, bf16[1024,384]{1,0:T(8,128)(2,1)}, u32[]{:S(2)}, u32[]{:S(2)}) collective-permute-start(bf16[1024,384]{1,0:T(8,128)(2,1)} %all_gather.7.y2), channel_id=1, source_target_pairs={{0,16},{1,17},{2,18},{3,19},{4,20},{5,21},{6,22},{7,23},{8,24},{9,... | collective-permute-start | bytes 2359304 | tf_op jit(solution)/shard_map/ppermute | solution.py:28
  72.8 6.4 %collective-permute-start.3 = (bf16[1024,384]{1,0:T(8,128)(2,1)S(1)}, bf16[1024,384]{1,0:T(8,128)(2,1)}, u32[]{:S(2)}, u32[]{:S(2)}) collective-permute-start(bf16[1024,384]{1,0:T(8,128)(2,1)S(1)} %all_gather.6.y0), channel_id=1, source_target_pairs={{0,16},{1,17},{2,18},{3,19},{4,20},{5,21},{6,22},{7,23},{8,24},{9,... | collective-permute-start | bytes 2359304 | tf_op jit(solution)/shard_map/ppermute | solution.py:28
  74.8 4.6 %collective-permute-start.5 = (bf16[1024,384]{1,0:T(8,128)(2,1)}, bf16[1024,384]{1,0:T(8,128)(2,1)}, u32[]{:S(2)}, u32[]{:S(2)}) collective-permute-start(bf16[1024,384]{1,0:T(8,128)(2,1)} %collective-permute-done.1.x1), channel_id=1, source_target_pairs={{0,16},{1,17},{2,18},{3,19},{4,20},{5,21},{6,22},{7,23},{8,24},{9,... | collective-permute-start | bytes 2359304 | tf_op jit(solution)/shard_map/ppermute | solution.py:28
  77.2 4.5 %collective-permute-start.6 = (bf16[1024,384]{1,0:T(8,128)(2,1)}, bf16[1024,384]{1,0:T(8,128)(2,1)}, u32[]{:S(2)}, u32[]{:S(2)}) collective-permute-start(bf16[1024,384]{1,0:T(8,128)(2,1)} %collective-permute-done.2.x3), channel_id=1, source_target_pairs={{0,16},{1,17},{2,18},{3,19},{4,20},{5,21},{6,22},{7,23},{8,24},{9,... | collective-permute-start | bytes 2359304 | tf_op jit(solution)/shard_map/ppermute | solution.py:28
